TPU v7x, 32 devices: a whole 2x2x4 slice. The times are simulated.
32 devices in a mesh: section: 8 (over z, x), fsdp: 4 (over y, core).
Axes of the slice: x: 2, y: 2, z: 4, core: 2. Of those that a mesh axis runs over, the one named last changes fastest.
Arguments:
- x_fwd: bfloat16 [8, 384, 4096], P('section', None, 'fsdp'), may hold values from -6 to 6
- x_saved: bfloat16 [8, 384, 4096], P('section', None, 'fsdp'), may hold values from -6 to 6
- cotangent: bfloat16 [8, 384, 4096], P('section', None, 'fsdp'), may hold values from -6 to 6
- qkv_weight: bfloat16 [8, 4096, 3, 4096], P('section', None, None, 'fsdp')
- gain: float32 [8, 4096], P('section', 'fsdp'), may hold values from 0.1 to 1.9
- block_lists: int32 [8, 3, 2], replicated, may hold values from 0 to 2, as said below
- plan: int32 [8, 2], P('section'), may hold values from 0 to 7
Outputs:
- y_next: bfloat16 [8, 384, 4096], P('section', None, 'fsdp')
- dx_prev: bfloat16 [8, 384, 4096], P('section', None, 'fsdp')
- w_grad: bfloat16 [8, 4096, 3, 4096], P('section', None, None, 'fsdp')
- gain_grad: float32 [8, 4096], P('section', 'fsdp')
Inputs may be any that keep to these rules, and one draw needn't show every extreme that they name: block_lists[z, b, 0] = b; the 2 entries of a row are distinct.
All inputs are finite; a program needn't handle non-finite values.
Results may differ from a plain program's by a relative error of at most 0.024.
Values may be sent and summed in bfloat16 or wider, within the bound.
A program may use at most 128 MiB of HBM per device.

v0:
```python
import math

import jax
import jax.numpy as jnp
from jax import lax
from jax.experimental import pallas as pl
from jax.experimental.pallas import tpu as pltpu
from jax.sharding import PartitionSpec as P

HD = 128
BLK = 128
EPS = 1e-05
INV = 1.0 / math.sqrt(HD)
VMEM = 40 * 1024 * 1024
F32 = jnp.float32
BF16 = jnp.bfloat16
NT = (((1,), (1,)), ((), ()))
TN = (((0,), (0,)), ((), ()))


def params(*sem):
    return pltpu.CompilerParams(dimension_semantics=sem, vmem_limit_bytes=VMEM)


def project_body(x_ref, w_ref, scale_ref, out_ref):
    product = jnp.dot(x_ref[...], w_ref[0], preferred_element_type=F32)
    out_ref[0] = (scale_ref[...] * product).astype(BF16)


def project(x, w3, scale):
    tokens, width = x.shape
    local = w3.shape[2]
    nt = min(256, local)
    return pl.pallas_call(
        project_body,
        grid=(3, local // nt),
        in_specs=[
            pl.BlockSpec((tokens, width), lambda k, j: (0, 0)),
            pl.BlockSpec((1, width, nt), lambda k, j: (k, 0, j)),
            pl.BlockSpec((tokens, 1), lambda k, j: (0, 0)),
        ],
        out_specs=pl.BlockSpec((1, tokens, nt), lambda k, j: (k, 0, j)),
        out_shape=jax.ShapeDtypeStruct((3, tokens, local), BF16),
        compiler_params=params("arbitrary", "arbitrary"),
        cost_estimate=pl.CostEstimate(
            flops=6 * tokens * width * local, bytes_accessed=6 * width * local, transcendentals=0
        ),
    )(x, w3, scale)


def probs_of(q_b, key, allowed):
    scores = lax.dot_general(q_b, key, NT, preferred_element_type=F32) * INV
    scores = jnp.where(allowed > 0.0, scores, -jnp.inf)
    expd = jnp.exp(scores - jnp.max(scores, axis=1, keepdims=True))
    return expd * (1.0 / jnp.sum(expd, axis=1, keepdims=True))


def forward_body(allow_ref, q_ref, k_ref, v_ref, x_ref, out_ref):
    tokens, cols = x_ref.shape
    for h in range(cols // HD):
        hs = slice(h * HD, (h + 1) * HD)
        key, value = k_ref[0, :, hs], v_ref[0, :, hs]
        for b in range(tokens // BLK):
            bs = slice(b * BLK, (b + 1) * BLK)
            low = probs_of(q_ref[0, bs, hs], key, allow_ref[b : b + 1, :]).astype(BF16)
            attn = jnp.dot(low, value, preferred_element_type=F32)
            out_ref[bs, hs] = (x_ref[bs, hs].astype(F32) + attn).astype(BF16)


def backward_body(allow_ref, q_ref, k_ref, v_ref, c_ref, scale_ref, grads_ref, total_ref):
    tokens, cols = c_ref.shape

    @pl.when(pl.program_id(0) == 0)
    def _():
        total_ref[...] = jnp.zeros_like(total_ref)

    for h in range(cols // HD):
        hs = slice(h * HD, (h + 1) * HD)
        key, value = k_ref[0, :, hs], v_ref[0, :, hs]
        grad_k = jnp.zeros((tokens, HD), F32)
        grad_v = jnp.zeros((tokens, HD), F32)
        for b in range(tokens // BLK):
            bs = slice(b * BLK, (b + 1) * BLK)
            q_b, c_b = q_ref[0, bs, hs], c_ref[bs, hs]
            probs = probs_of(q_b, key, allow_ref[b : b + 1, :])
            grad_v += lax.dot_general(probs.astype(BF16), c_b, TN, preferred_element_type=F32)
            grad_p = lax.dot_general(c_b, value, NT, preferred_element_type=F32)
            inner = jnp.sum(probs * grad_p, axis=1, keepdims=True)
            low = (probs * (grad_p - inner) * INV).astype(BF16)
            grad_k += lax.dot_general(low, q_b, TN, preferred_element_type=F32)
            grad_q = scale_ref[bs, :] * jnp.dot(low, key, preferred_element_type=F32)
            grad_q = grad_q.astype(BF16)
            grads_ref[0, bs, hs] = grad_q
            total_ref[bs, :] += grad_q.astype(F32) * q_b.astype(F32)
        grad_k = (scale_ref[...] * grad_k).astype(BF16)
        grad_v = (scale_ref[...] * grad_v).astype(BF16)
        grads_ref[1, :, hs] = grad_k
        grads_ref[2, :, hs] = grad_v
        total_ref[...] += grad_k.astype(F32) * key.astype(F32) + grad_v.astype(F32) * value.astype(F32)


def attention_specs(tokens, hw):
    part = lambda k: pl.BlockSpec((1, tokens, hw), lambda h: (k, 0, h))
    return [
        pl.BlockSpec((tokens // BLK, tokens), lambda h: (0, 0)),
        part(0),
        part(1),
        part(2),
        pl.BlockSpec((tokens, hw), lambda h: (0, h)),
    ]


def attend_forward(allowed, proj, x):
    tokens, local = x.shape
    hw = min(2 * HD, local)
    return pl.pallas_call(
        forward_body,
        grid=(local // hw,),
        in_specs=attention_specs(tokens, hw),
        out_specs=pl.BlockSpec((tokens, hw), lambda h: (0, h)),
        out_shape=jax.ShapeDtypeStruct((tokens, local), BF16),
        compiler_params=params("arbitrary"),
        cost_estimate=pl.CostEstimate(
            flops=16 * tokens * tokens * local, bytes_accessed=10 * tokens * local, transcendentals=0
        ),
    )(allowed, proj, proj, proj, x)


def attend_backward(allowed, proj, c, scale):
    tokens, local = c.shape
    hw = min(2 * HD, local)
    return pl.pallas_call(
        backward_body,
        grid=(local // hw,),
        in_specs=attention_specs(tokens, hw) + [pl.BlockSpec((tokens, 1), lambda h: (0, 0))],
        out_specs=[
            pl.BlockSpec((3, tokens, hw), lambda h: (0, 0, h)),
            pl.BlockSpec((tokens, HD), lambda h: (0, 0)),
        ],
        out_shape=[
            jax.ShapeDtypeStruct((3, tokens, local), BF16),
            jax.ShapeDtypeStruct((tokens, HD), F32),
        ],
        compiler_params=params("arbitrary"),
        cost_estimate=pl.CostEstimate(
            flops=40 * tokens * tokens * local, bytes_accessed=14 * tokens * local, transcendentals=0
        ),
    )(allowed, proj, proj, proj, c, scale)


def grad_in_body(ids_ref, grads_ref, w_ref, out_ref):
    total = lax.dot_general(grads_ref[0], w_ref[0], NT, preferred_element_type=F32)
    for k in (1, 2):
        total += lax.dot_general(grads_ref[k], w_ref[k], NT, preferred_element_type=F32)
    out_ref[0] = total.astype(out_ref.dtype)


def grad_in_blocks(ids, grads, w3, out_type):
    tokens, local = grads.shape[1:]
    count = ids.shape[0]
    ft = min(512, local)
    steps = local // ft
    return pl.pallas_call(
        grad_in_body,
        grid_spec=pltpu.PrefetchScalarGridSpec(
            num_scalar_prefetch=1,
            grid=(count, steps),
            in_specs=[
                pl.BlockSpec((3, tokens, local), lambda i, j, ids: (0, 0, 0)),
                pl.BlockSpec((3, ft, local), lambda i, j, ids: (0, ids[i] * steps + j, 0)),
            ],
            out_specs=pl.BlockSpec((1, tokens, ft), lambda i, j, ids: (i, 0, j)),
        ),
        out_shape=jax.ShapeDtypeStruct((count, tokens, local), out_type),
        compiler_params=params("arbitrary", "arbitrary"),
        cost_estimate=pl.CostEstimate(
            flops=6 * tokens * count * local * local,
            bytes_accessed=6 * count * local * local,
            transcendentals=0,
        ),
    )(ids, grads, w3)


def grad_w_body(x_ref, grads_ref, out_ref):
    flipped = x_ref[...].T
    for k in range(3):
        out_ref[k] = jnp.dot(flipped, grads_ref[k], preferred_element_type=F32).astype(BF16)


def grad_weight(x, grads):
    tokens, width = x.shape
    local = grads.shape[2]
    ft = 512
    return pl.pallas_call(
        grad_w_body,
        grid=(width // ft,),
        in_specs=[
            pl.BlockSpec((tokens, ft), lambda j: (0, j)),
            pl.BlockSpec((3, tokens, local), lambda j: (0, 0, 0)),
        ],
        out_specs=pl.BlockSpec((3, ft, local), lambda j: (0, j, 0)),
        out_shape=jax.ShapeDtypeStruct((3, width, local), BF16),
        compiler_params=params("arbitrary"),
        cost_estimate=pl.CostEstimate(
            flops=6 * tokens * width * local, bytes_accessed=6 * width * local, transcendentals=0
        ),
    )(x, grads)


def shifted(block, axis, distance):
    n = lax.axis_size(axis)
    return lax.ppermute(block, axis, [((i - distance) % n, i) for i in range(n)])


def allowed_keys(ids, tokens):
    blocks = jnp.arange(tokens, dtype=jnp.int32) // BLK
    return jnp.any(ids[:, :, None] == blocks[None, None, :], axis=1).astype(F32)


def on_device(x_fwd, x_saved, cotangent, qkv_weight, gain, block_lists, plan):
    forward_in, saved_in, upstream = x_fwd[0], x_saved[0], cotangent[0]
    gain_row = gain[0][None, :]
    w3 = jnp.transpose(qkv_weight[0], (1, 0, 2))
    full_width, local = w3.shape[1:]
    tokens = forward_in.shape[0]
    n = lax.axis_size("fsdp")
    chips = n // 2
    me = lax.axis_index("fsdp")
    chip, core = me // 2, me % 2

    wide_fwd = forward_in.astype(F32)
    wide_bwd = saved_in.astype(F32)
    scaled_bwd = (wide_bwd * gain_row).astype(BF16)
    scaled_fwd = (wide_fwd * gain_row).astype(BF16)
    squares = jnp.stack([jnp.sum(wide_fwd * wide_fwd, axis=1), jnp.sum(wide_bwd * wide_bwd, axis=1)])
    whole_bwd = lax.all_gather(scaled_bwd, "fsdp", axis=1, tiled=True)
    squares = jnp.sum(lax.all_gather(squares, "fsdp"), axis=0)
    whole_fwd = lax.all_gather(scaled_fwd, "fsdp", axis=1, tiled=True)
    scales = lax.rsqrt(squares / full_width + EPS)
    scale_fwd, scale_bwd = scales[0][:, None], scales[1][:, None]

    proj_bwd = project(whole_bwd, w3, scale_bwd)
    allowed_bwd = allowed_keys(block_lists[plan[0, 1]], tokens)
    grads, totals = attend_backward(allowed_bwd, proj_bwd, upstream, scale_bwd)
    totals = jnp.sum(lax.all_gather(jnp.sum(totals, axis=1), "fsdp"), axis=0)

    others = jnp.arange(chips, dtype=jnp.int32)
    theirs = grad_in_blocks(others * 2 + 1 - core, grads, w3, BF16)
    from_core = lax.ppermute(theirs, "fsdp", [(i, i ^ 1) for i in range(n)])
    far = (chip + 1 + jnp.arange(chips - 1, dtype=jnp.int32)) % chips
    far_part = grad_in_blocks(far * 2 + core, grads, w3, F32)
    arrived = []
    for d in range(1, chips):
        here = lax.dynamic_index_in_dim(from_core, (chip + d) % chips, 0, keepdims=False)
        send = (far_part[d - 1] + here.astype(F32)).astype(BF16)
        route = [(i, ((i // 2 + d) % chips) * 2 + i % 2) for i in range(n)]
        arrived.append(lax.ppermute(send, "fsdp", route))
    own_in = grad_in_blocks(me[None].astype(jnp.int32), grads, w3, F32)[0]
    own_in += lax.dynamic_index_in_dim(from_core, chip, 0, keepdims=False).astype(F32)

    proj_fwd = project(whole_fwd, w3, scale_fwd)
    allowed_fwd = allowed_keys(block_lists[plan[0, 0]], tokens)
    result = attend_forward(allowed_fwd, proj_fwd, forward_in)
    sent_on = shifted(result[None], "section", 1)

    for block in arrived:
        own_in += block.astype(F32)
    grad_x = upstream.astype(F32) + gain_row * own_in
    grad_x = grad_x - scale_bwd * (totals / full_width)[:, None] * wide_bwd
    sent_back = shifted(grad_x.astype(BF16)[None], "section", -1)
    grad_gain = jnp.sum(wide_bwd * own_in, axis=0)[None]
    grad_w = jnp.transpose(grad_weight(whole_bwd, grads), (1, 0, 2))[None]
    return (sent_on, sent_back, grad_w, grad_gain)


def solution(mesh):
    in_specs = (
        P("section", None, "fsdp"),
        P("section", None, "fsdp"),
        P("section", None, "fsdp"),
        P("section", None, None, "fsdp"),
        P("section", "fsdp"),
        P(),
        P("section", None),
    )
    out_specs = (
        P("section", None, "fsdp"),
        P("section", None, "fsdp"),
        P("section", None, None, "fsdp"),
        P("section", "fsdp"),
    )
    return jax.shard_map(
        on_device, mesh=mesh, in_specs=in_specs, out_specs=out_specs, check_vma=False
    )
```

profile of v0, /device:TPU:0, one launch (start us, length us, event | category | flops | bytes accessed | tf_op | source)
XLA Modules:
  0.0 169.6 jit_solution(1701102757424400251)
XLA Ops:
  7.2 2.8 %fusion.1 = (f32[384]{0:T(512)S(1)}, bf16[384,1024]{1,0:T(8,128)(2,1)}, f32[384]{0:T(512)S(1)}, bf16[384,1024]{1,0:T(8,128)(2,1)}) fusion(bf16[1,384,1024]{2,1,0:T(8,128)(2,1)} %param.7, f32[1024]{0:T(1024)} %bitcast.50, bf16[1,384,1024]{2,1,0:T(8,128)(2,1)} %param.8), kind=kLoop, calls=%fused_computation.7 | loop fusion | flops 3931392 | bytes 3152896 | tf_op jit(solution)/shard_map/reduce_sum | solution.py:235
  10.1 0.7 all-gather.7.cloned.1.call-update
  10.8 0.6 fusion.12
  15.7 6.2 %all-gather.2 = f32[4,2,384]{2,1,0:T(2,128)S(1)} all-gather(f32[1,2,384]{2,1,0:T(2,128)S(1)} %maximum_bitcast_fusion), channel_id=2, replica_groups=mesh['section'=8,'fsdp'=4] {'fsdp'}, dimensions={0}, use_global_device_ids=true | all-gather | bytes 15360 | tf_op jit(solution)/shard_map/all_gather | solution.py:237
  22.1 19.3 %all-gather.9.cloned.1.call-done.x_ref = bf16[384,4096]{1,0:T(8,128)(2,1)} async-done(((bf16[384,1024]{1,0:T(8,128)(2,1)}), bf16[384,4096]{1,0:T(8,128)(2,1)}) %all-gather.9.cloned.1.call-update) | async-done | bytes 3145744 | tf_op jit(solution)/shard_map/all_gather | solution.py:236
  41.5 1.9 %copy-done.3 = bf16[384,4096]{1,0:T(8,128)(2,1)S(1)} copy-done((bf16[384,4096]{1,0:T(8,128)(2,1)S(1)}, bf16[384,4096]{1,0:T(8,128)(2,1)}, u32[]{:S(2)}) %copy-start.3) | copy-done | bytes 3145752
  43.3 17.6 %shard_map.104.q_ref.k_ref.v_ref = bf16[3,384,1024]{2,1,0:T(8,128)(2,1)S(1)} custom-call(bf16[384,4096]{1,0:T(8,128)(2,1)S(1)} %copy-done.3, bf16[3,4096,1024]{2,1,0:T(8,128)(2,1)} %bitcast.45, f32[384,1]{1,0:T(8,128)S(1)} %copy.32.scale_ref), custom_call_target="tpu_custom_call" | custom-call | flops 9663676416 | bytes 25165824 | tf_op jit(solution)/shard_map/pallas_call | solution.py:34
  61.0 14.2 %shard_map.105 = (bf16[3,384,1024]{2,1,0:T(8,128)(2,1)S(1)}, f32[384,128]{1,0:T(8,128)S(1)}) custom-call(f32[3,384]{1,0:T(4,128)S(1)} %convert_element_type.50.allow_ref, bf16[3,384,1024]{2,1,0:T(8,128)(2,1)S(1)} %shard_map.104.q_ref.k_ref.v_ref, bf16[3,384,1024]{2,1,0:T(8,128)(2,1)S(1)} %shard_map.104.q_ref.k_ref.v_ref, ...), custom_call_target="tpu_custom_call" | custom-call | flops 6039797760 | bytes 5505024 | tf_op jit(solution)/shard_map/pallas_call | solution.py:132
  75.2 9.7 %shard_map.107 = bf16[2,384,1024]{2,1,0:T(8,128)(2,1)} custom-call(s32[2]{0:T(128)S(1)} %add_subtract_fusion.ids_ref, bf16[3,384,1024]{2,1,0:T(8,128)(2,1)S(1)} %get-tuple-element.6.grads_ref, bf16[3,4096,1024]{2,1,0:T(8,128)(2,1)} %bitcast.46), custom_call_target="tpu_custom_call" | custom-call | flops 4831838208 | bytes 12582912 | tf_op jit(solution)/shard_map/pallas_call | solution.py:163
  85.3 4.8 %shard_map.108 = f32[1,384,1024]{2,1,0:T(8,128)S(1)} custom-call(s32[1]{0:T(128)S(6)} %add.83.ids_ref, bf16[3,384,1024]{2,1,0:T(8,128)(2,1)S(1)} %get-tuple-element.6.grads_ref, bf16[3,4096,1024]{2,1,0:T(8,128)(2,1)} %bitcast.47), custom_call_target="tpu_custom_call" | custom-call | flops 2415919104 | bytes 6291456 | tf_op jit(solution)/shard_map/pallas_call | solution.py:163
  90.2 2.3 %fusion.7 = bf16[384,1024]{1,0:T(8,128)(2,1)} fusion(f32[1,384,1024]{2,1,0:T(8,128)S(1)} %shard_map.108, bf16[2,384,1024]{2,1,0:T(8,128)(2,1)} %collective-permute-done.1, s32[]{:T(128)S(6)} %select_n.54), kind=kLoop, calls=%fused_computation.15 | loop fusion | flops 1179648 | bytes 3145732 | tf_op jit(solution)/shard_map/convert_element_type | solution.py:255
  92.8 1.9 %copy-done.5 = bf16[384,4096]{1,0:T(8,128)(2,1)S(1)} copy-done((bf16[384,4096]{1,0:T(8,128)(2,1)S(1)}, bf16[384,4096]{1,0:T(8,128)(2,1)}, u32[]{:S(2)}) %copy-start.5) | copy-done | bytes 3145752
  94.7 17.1 %shard_map.102.q_ref.k_ref.v_ref = bf16[3,384,1024]{2,1,0:T(8,128)(2,1)S(1)} custom-call(bf16[384,4096]{1,0:T(8,128)(2,1)S(1)} %copy-done.5, bf16[3,4096,1024]{2,1,0:T(8,128)(2,1)} %bitcast.48, f32[384,1]{1,0:T(8,128)S(1)} %copy.30.scale_ref), custom_call_target="tpu_custom_call" | custom-call | flops 9663676416 | bytes 25165824 | tf_op jit(solution)/shard_map/pallas_call | solution.py:34
  111.9 9.9 %shard_map.103 = bf16[384,1024]{1,0:T(8,128)(2,1)} custom-call(f32[3,384]{1,0:T(4,128)S(1)} %convert_element_type.44.allow_ref, bf16[3,384,1024]{2,1,0:T(8,128)(2,1)S(1)} %shard_map.102.q_ref.k_ref.v_ref, bf16[3,384,1024]{2,1,0:T(8,128)(2,1)S(1)} %shard_map.102.q_ref.k_ref.v_ref, bf16[3,384,1024]{2,1,0:T(8,128)(2,1)S(1)} %shard_map.102.q_ref.k_ref.v_ref, ...), custom_call_target="tpu_custom_call" | custom-call | flops 2415919104 | bytes 3932160 | tf_op jit(solution)/shard_map/pallas_call | solution.py:116
  121.8 1.7 %collective-permute-start = (bf16[1,384,1024]{2,1,0:T(8,128)(2,1)}, bf16[1,384,1024]{2,1,0:T(8,128)(2,1)S(1)}, u32[]{:S(2)}, u32[]{:S(2)}) collective-permute-start(bf16[1,384,1024]{2,1,0:T(8,128)(2,1)} %bitcast.9), channel_id=1, source_target_pairs={{28,0},{0,4},{4,8},{8,12},{12,16},{16,20},{20,24},{24,28},{29,1},{... | collective-permute-start | bytes 2359304 | tf_op jit(solution)/shard_map/ppermute | solution.py:212
  123.6 5.2 %all-gather.3 = f32[4,1,384]{2,1,0:T(1,128)S(1)} all-gather(f32[1,1,384]{2,1,0:T(1,128)S(1)} %reshape.47), channel_id=3, replica_groups=mesh['section'=8,'fsdp'=4] {'fsdp'}, dimensions={0}, use_global_device_ids=true | all-gather | bytes 7680 | tf_op jit(solution)/shard_map/all_gather | solution.py:245
  128.9 5.0 %shard_map.106 = f32[1,384,1024]{2,1,0:T(8,128)S(1)} custom-call(s32[1]{0:T(128)} %bitcast.11.ids_ref, bf16[3,384,1024]{2,1,0:T(8,128)(2,1)S(1)} %get-tuple-element.6.grads_ref, bf16[3,4096,1024]{2,1,0:T(8,128)(2,1)} %bitcast.49), custom_call_target="tpu_custom_call" | custom-call | flops 2415919104 | bytes 6291456 | tf_op jit(solution)/shard_map/pallas_call | solution.py:163
  133.9 2.8 %fusion.6 = (f32[1024]{0:T(1024)}, bf16[1,384,1024]{2,1,0:T(8,128)(2,1)S(1)}) fusion(bf16[1,384,1024]{2,1,0:T(8,128)(2,1)S(1)} %copy-done.6, bf16[384,1024]{1,0:T(8,128)(2,1)} %collective-permute-done.2, f32[1,384,1024]{2,1,0:T(8,128)S(1)} %shard_map.106, bf16[2,384,1024]{2,1,0:T(8,128)(2,1)} %collective-permute-done.1, s32[]{:T(128)S(6)} %select_n.51, ...), kind=kLoop, calls=%fused_computation.12 | loop fusion | flops 5110784 | bytes 5514756 | tf_op jit(solution)/shard_map/reduce_sum | solution.py:271
  136.7 3.0 %collective-permute-start.3 = (bf16[1,384,1024]{2,1,0:T(8,128)(2,1)S(1)}, bf16[1,384,1024]{2,1,0:T(8,128)(2,1)S(1)}, u32[]{:S(2)}, u32[]{:S(2)}) collective-permute-start(bf16[1,384,1024]{2,1,0:T(8,128)(2,1)S(1)} %get-tuple-element.11), channel_id=1, source_target_pairs={{4,0},{8,4},{12,8},{16,12},{20,16},{24,20},{28,24},{0,28},{5,1},{9... | collective-permute-start | bytes 2359304 | tf_op jit(solution)/shard_map/ppermute | solution.py:212
  139.7 16.6 %shard_map.109 = bf16[3,4096,1024]{2,1,0:T(8,128)(2,1)} custom-call(bf16[384,4096]{1,0:T(8,128)(2,1)S(1)} %copy-done.4, bf16[3,384,1024]{2,1,0:T(8,128)(2,1)S(1)} %get-tuple-element.6.grads_ref), custom_call_target="tpu_custom_call" | custom-call | flops 9663676416 | bytes 25165824 | tf_op jit(solution)/shard_map/pallas_call | solution.py:194
  156.4 1.3 collective-permute-done
  157.6 3.4 %collective-permute-done.3 = bf16[1,384,1024]{2,1,0:T(8,128)(2,1)S(1)} collective-permute-done((bf16[1,384,1024]{2,1,0:T(8,128)(2,1)S(1)}, bf16[1,384,1024]{2,1,0:T(8,128)(2,1)S(1)}, u32[]{:S(2)}, u32[]{:S(2)}) %collective-permute-start.3) | collective-permute-done | bytes 786464 | tf_op jit(solution)/shard_map/ppermute | solution.py:212
  161.0 0.9 copy.36
  161.9 0.9 copy.37
  (46 shorter events, 1.7 us)
Async XLA Ops:
  7.2 34.3 %all-gather.9.cloned.1.call-start = ((), (), s32[]{:S(2)}) async-start(), calls=%async_computation.1 | async-start | bytes 3932160 | tf_op jit(solution)/shard_map/all_gather | solution.py:236
  10.0 0.8 copy-start.9
  10.0 5.3 %copy-start.8 = (s32[8,3,2]{0,2,1:T(2,128)S(1)}, s32[8,3,2]{0,2,1:T(2,128)}, u32[]{:S(2)}) copy-start(s32[8,3,2]{0,2,1:T(2,128)} %param.12) | copy-start | bytes 580
  10.1 82.8 %all-gather.7.cloned.1.call-start = ((), (), s32[]{:S(2)}) async-start(), calls=%async_computation | async-start | bytes 3932160 | tf_op jit(solution)/shard_map/all_gather | solution.py:238
  41.5 1.9 %copy-start.3 = (bf16[384,4096]{1,0:T(8,128)(2,1)S(1)}, bf16[384,4096]{1,0:T(8,128)(2,1)}, u32[]{:S(2)}) copy-start(bf16[384,4096]{1,0:T(8,128)(2,1)} %all-gather.9.cloned.1.call-done.x_ref) | copy-start | bytes 9437188
  43.3 17.6 %copy-start.1 = (bf16[1,384,1024]{2,1,0:T(8,128)(2,1)S(1)}, bf16[1,384,1024]{2,1,0:T(8,128)(2,1)}, u32[]{:S(2)}) copy-start(bf16[1,384,1024]{2,1,0:T(8,128)(2,1)} %param.9) | copy-start | bytes 2359300
  84.9 5.3 %collective-permute-start.1 = (bf16[2,384,1024]{2,1,0:T(8,128)(2,1)}, bf16[2,384,1024]{2,1,0:T(8,128)(2,1)}, u32[]{:S(2)}, u32[]{:S(2)}) collective-permute-start(bf16[2,384,1024]{2,1,0:T(8,128)(2,1)} %shard_map.107), channel_id=1, source_target_pairs={{0,1},{1,0},{2,3},{3,2},{4,5},{5,4},{6,7},{7,6},{8,9},{9,8},{10,11... | collective-permute-start | bytes 4718600 | tf_op jit(solution)/shard_map/ppermute | solution.py:249
  92.5 19.4 %copy-start = (bf16[1,384,1024]{2,1,0:T(8,128)(2,1)S(1)}, bf16[1,384,1024]{2,1,0:T(8,128)(2,1)}, u32[]{:S(2)}) copy-start(bf16[1,384,1024]{2,1,0:T(8,128)(2,1)} %param.7) | copy-start | bytes 2359300
  92.5 41.4 %collective-permute-start.2 = (bf16[384,1024]{1,0:T(8,128)(2,1)}, bf16[384,1024]{1,0:T(8,128)(2,1)}, u32[]{:S(2)}, u32[]{:S(2)}) collective-permute-start(bf16[384,1024]{1,0:T(8,128)(2,1)} %fusion.7), channel_id=1, source_target_pairs={{0,2},{1,3},{2,0},{3,1},{4,6},{5,7},{6,4},{7,5},{8,10},{9,11},{10,... | collective-permute-start | bytes 2359304 | tf_op jit(solution)/shard_map/ppermute | solution.py:257
  92.8 1.9 %copy-start.5 = (bf16[384,4096]{1,0:T(8,128)(2,1)S(1)}, bf16[384,4096]{1,0:T(8,128)(2,1)}, u32[]{:S(2)}) copy-start(bf16[384,4096]{1,0:T(8,128)(2,1)} %all-gather.7.cloned.1.call-done.x_ref) | copy-start | bytes 9437188
  121.8 35.9 %collective-permute-start = (bf16[1,384,1024]{2,1,0:T(8,128)(2,1)}, bf16[1,384,1024]{2,1,0:T(8,128)(2,1)S(1)}, u32[]{:S(2)}, u32[]{:S(2)}) collective-permute-start(bf16[1,384,1024]{2,1,0:T(8,128)(2,1)} %bitcast.9), channel_id=1, source_target_pairs={{28,0},{0,4},{4,8},{8,12},{12,16},{16,20},{20,24},{24,28},{29,1},{... | collective-permute-start | bytes 2359304 | tf_op jit(solution)/shard_map/ppermute | solution.py:212
  128.8 5.0 %copy-start.2 = (bf16[1,384,1024]{2,1,0:T(8,128)(2,1)S(1)}, bf16[1,384,1024]{2,1,0:T(8,128)(2,1)}, u32[]{:S(2)}) copy-start(bf16[1,384,1024]{2,1,0:T(8,128)(2,1)} %param.9) | copy-start | bytes 2359300
  128.8 5.0 %copy-start.6 = (bf16[1,384,1024]{2,1,0:T(8,128)(2,1)S(1)}, bf16[1,384,1024]{2,1,0:T(8,128)(2,1)}, u32[]{:S(2)}) copy-start(bf16[1,384,1024]{2,1,0:T(8,128)(2,1)} %param.8) | copy-start | bytes 2359300
  128.8 5.0 %copy-start.7 = (f32[1,1024]{1,0:T(1,128)S(1)}, f32[1,1024]{1,0:T(1,128)}, u32[]{:S(2)}) copy-start(f32[1,1024]{1,0:T(1,128)} %param.11) | copy-start | bytes 12292
  133.8 5.9 %copy-start.4 = (bf16[384,4096]{1,0:T(8,128)(2,1)S(1)}, bf16[384,4096]{1,0:T(8,128)(2,1)}, u32[]{:S(2)}) copy-start(bf16[384,4096]{1,0:T(8,128)(2,1)} %all-gather.9.cloned.1.call-done.x_ref) | copy-start | bytes 9437188
  136.7 24.3 %collective-permute-start.3 = (bf16[1,384,1024]{2,1,0:T(8,128)(2,1)S(1)}, bf16[1,384,1024]{2,1,0:T(8,128)(2,1)S(1)}, u32[]{:S(2)}, u32[]{:S(2)}) collective-permute-start(bf16[1,384,1024]{2,1,0:T(8,128)(2,1)S(1)} %get-tuple-element.11), channel_id=1, source_target_pairs={{4,0},{8,4},{12,8},{16,12},{20,16},{24,20},{28,24},{0,28},{5,1},{9... | collective-permute-start | bytes 2359304 | tf_op jit(solution)/shard_map/ppermute | solution.py:212
Sparse Core Ops, SparseCore 0:
  10.2 31.2 all-gather.8
  43.6 28.5 all-gather.6
where the time goes:
time: 170 us
  Pallas kernels  95 us (56%)
  waiting for transfers between devices  24.7 us (15%)
  between operations  18.2 us (11%)
  blocking collectives  11.3 us (7%)
  other arithmetic  8.23 us (5%)
  local copies, waits for them, and re-layouts  6.74 us (4%)
  starting transfers between devices  5.45 us (3%)
    pallas_call x2, Pallas kernels, project(): pl.pallas_call(project_body, grid=(3, local // nt), in_specs=[pl.BlockSpe...  34.7 us
    pallas_call x3, Pallas kernels, grad_in_blocks(): pl.pallas_call(grad_in_body, grid_spec=pltpu.PrefetchScalarGridSpec(num_s...  19.5 us
    all_gather x1, waiting for transfers between devices, on_device(): whole_bwd = lax.all_gather(scaled_bwd, 'fsdp', axis=1, tiled=True)  19.3 us
    pallas_call x1, Pallas kernels, grad_weight(): pl.pallas_call(grad_w_body, grid=(width // ft,), in_specs=[pl.BlockSpec((...  16.6 us
    pallas_call x1, Pallas kernels, attend_backward(): pl.pallas_call(backward_body, grid=(local // hw,), in_specs=attention_spe...  14.2 us
    pallas_call x1, Pallas kernels, attend_forward(): pl.pallas_call(forward_body, grid=(local // hw,), in_specs=attention_spec...  9.91 us
    all_gather x1, blocking collectives, on_device(): squares = jnp.sum(lax.all_gather(squares, 'fsdp'), axis=0)  6.19 us
    unnamed x23, local copies, waits for them, and re-layouts  5.58 us
  transfers between devices with their start and end apart: 6, of which 3 were waited for; matrix products, arithmetic and copies ran while one was open for 4% of the time, Pallas kernels for 56%

commit v1 on v0

v1 whole, which is shorter than its diff:
```python
import math

import jax
import jax.numpy as jnp
from jax import lax
from jax.experimental import pallas as pl
from jax.experimental.pallas import tpu as pltpu
from jax.sharding import PartitionSpec as P

HD = 128
BLK = 128
EPS = 1e-05
INV = 1.0 / math.sqrt(HD)
LOG2E = math.log2(math.e)
VMEM = 40 * 1024 * 1024
F32 = jnp.float32
BF16 = jnp.bfloat16
NT = (((1,), (1,)), ((), ()))
TN = (((0,), (0,)), ((), ()))


def cost(flops, moved):
    return pl.CostEstimate(flops=flops // 16, bytes_accessed=moved // 16, transcendentals=0)


def params(*sem):
    return pltpu.CompilerParams(dimension_semantics=sem, vmem_limit_bytes=VMEM)


def total_of(x_refs, w_refs):
    total = jnp.dot(x_refs[0][...], w_refs[0][0], preferred_element_type=F32)
    for x_ref, w_ref in zip(x_refs[1:], w_refs[1:]):
        total += jnp.dot(x_ref[...], w_ref[0], preferred_element_type=F32)
    return total


def near_body(ids_ref, *refs):
    count = (len(refs) - 1) // 2
    refs[-1][0] = total_of(refs[:count], refs[count:-1])


def far_body(ids_ref, *refs):
    acc_ref, scale_ref, out_ref = refs[-3:]
    count = (len(refs) - 3) // 2
    product = acc_ref[0] + total_of(refs[:count], refs[count:-3])
    out_ref[0] = (scale_ref[...] * product).astype(BF16)


def operand_specs(count, tokens, local, nt):
    specs = [pl.BlockSpec((tokens, local), lambda k, j, ids: (0, 0)) for _ in range(count)]
    for i in range(count):
        specs.append(pl.BlockSpec((1, local, nt), lambda k, j, ids, i=i: (k, ids[i], j)))
    return specs


def project_cost(tokens, count, local):
    return cost(6 * tokens * count * local * local, 6 * count * local * local)


def project_near(ids, blocks, w3):
    tokens, local = blocks[0].shape
    nt = min(256, local)
    count = len(blocks)
    return pl.pallas_call(
        near_body,
        grid_spec=pltpu.PrefetchScalarGridSpec(
            num_scalar_prefetch=1,
            grid=(3, local // nt),
            in_specs=operand_specs(count, tokens, local, nt),
            out_specs=pl.BlockSpec((1, tokens, nt), lambda k, j, ids: (k, 0, j)),
        ),
        out_shape=jax.ShapeDtypeStruct((3, tokens, local), F32),
        compiler_params=params("arbitrary", "arbitrary"),
        cost_estimate=project_cost(tokens, count, local),
    )(ids, *blocks, *[w3] * count)


def project_far(ids, blocks, w3, acc, half, scale):
    tokens, local = blocks[0].shape
    nt = min(256, local)
    count = len(blocks)
    return pl.pallas_call(
        far_body,
        grid_spec=pltpu.PrefetchScalarGridSpec(
            num_scalar_prefetch=1,
            grid=(3, local // nt),
            in_specs=operand_specs(count, tokens, local, nt)
            + [
                pl.BlockSpec((1, tokens, nt), lambda k, j, ids: (k, half, j)),
                pl.BlockSpec((tokens, 1), lambda k, j, ids: (0, 0)),
            ],
            out_specs=pl.BlockSpec((1, tokens, nt), lambda k, j, ids: (k, 0, j)),
        ),
        out_shape=jax.ShapeDtypeStruct((3, tokens, local), BF16),
        compiler_params=params("arbitrary", "arbitrary"),
        cost_estimate=project_cost(tokens, count, local),
    )(ids, *blocks, *[w3] * count, acc, scale)


def probs_of(q_b, key_a, key_b):
    s_a = lax.dot_general(key_a, q_b, NT, preferred_element_type=F32)
    s_b = lax.dot_general(key_b, q_b, NT, preferred_element_type=F32)
    top = jnp.max(jnp.maximum(s_a, s_b), axis=0, keepdims=True)
    e_a = jnp.exp2((s_a - top) * (INV * LOG2E))
    e_b = jnp.exp2((s_b - top) * (INV * LOG2E))
    share = 1.0 / jnp.sum(e_a + e_b, axis=0, keepdims=True)
    return e_a * share, e_b * share


def other_rows(ids_ref, b):
    return pl.ds(pl.multiple_of(ids_ref[b, 1] * BLK, BLK), BLK)


def forward_body(ids_ref, q_ref, k_ref, v_ref, x_ref, out_ref):
    tokens, cols = x_ref.shape
    for h in range(cols // HD):
        hs = slice(h * HD, (h + 1) * HD)
        for b in range(tokens // BLK):
            bs = slice(b * BLK, (b + 1) * BLK)
            other = other_rows(ids_ref, b)
            p_a, p_b = probs_of(q_ref[0, bs, hs], k_ref[0, bs, hs], k_ref[0, other, hs])
            attn = lax.dot_general(p_a.astype(BF16), v_ref[0, bs, hs], TN, preferred_element_type=F32)
            attn += lax.dot_general(
                p_b.astype(BF16), v_ref[0, other, hs], TN, preferred_element_type=F32
            )
            out_ref[bs, hs] = (x_ref[bs, hs].astype(F32) + attn).astype(BF16)


def backward_body(ids_ref, q_ref, k_ref, v_ref, c_ref, scale_ref, grads_ref, total_ref, gk_ref, gv_ref):
    tokens, cols = c_ref.shape

    @pl.when(pl.program_id(0) == 0)
    def _():
        total_ref[...] = jnp.zeros_like(total_ref)

    for h in range(cols // HD):
        hs = slice(h * HD, (h + 1) * HD)
        later = []
        for b in range(tokens // BLK):
            bs = slice(b * BLK, (b + 1) * BLK)
            other = other_rows(ids_ref, b)
            q_b, c_b = q_ref[0, bs, hs], c_ref[bs, hs]
            key_a, key_b = k_ref[0, bs, hs], k_ref[0, other, hs]
            p_a, p_b = probs_of(q_b, key_a, key_b)
            gp_a = lax.dot_general(v_ref[0, bs, hs], c_b, NT, preferred_element_type=F32)
            gp_b = lax.dot_general(v_ref[0, other, hs], c_b, NT, preferred_element_type=F32)
            inner = jnp.sum(p_a * gp_a + p_b * gp_b, axis=0, keepdims=True)
            gs_a = (p_a * (gp_a - inner) * INV).astype(BF16)
            gs_b = (p_b * (gp_b - inner) * INV).astype(BF16)
            gv_ref[h, bs, :] = jnp.dot(p_a.astype(BF16), c_b, preferred_element_type=F32)
            gk_ref[h, bs, :] = jnp.dot(gs_a, q_b, preferred_element_type=F32)
            later.append((other, p_b.astype(BF16), c_b, gs_b, q_b))
            grad_q = lax.dot_general(gs_a, key_a, TN, preferred_element_type=F32)
            grad_q += lax.dot_general(gs_b, key_b, TN, preferred_element_type=F32)
            grad_q = (scale_ref[bs, :] * grad_q).astype(BF16)
            grads_ref[0, bs, hs] = grad_q
            total_ref[bs, :] += grad_q.astype(F32) * q_b.astype(F32)
        for other, p_b, c_b, gs_b, q_b in later:
            gv_ref[h, other, :] += jnp.dot(p_b, c_b, preferred_element_type=F32)
            gk_ref[h, other, :] += jnp.dot(gs_b, q_b, preferred_element_type=F32)
        grad_k = (scale_ref[...] * gk_ref[h]).astype(BF16)
        grad_v = (scale_ref[...] * gv_ref[h]).astype(BF16)
        grads_ref[1, :, hs] = grad_k
        grads_ref[2, :, hs] = grad_v
        total_ref[...] += grad_k.astype(F32) * k_ref[0, :, hs].astype(F32)
        total_ref[...] += grad_v.astype(F32) * v_ref[0, :, hs].astype(F32)


def attention_specs(tokens, hw):
    part = lambda k: pl.BlockSpec((1, tokens, hw), lambda h, ids: (k, 0, h))
    return [part(0), part(1), part(2), pl.BlockSpec((tokens, hw), lambda h, ids: (0, h))]


def attend_forward(ids, proj, x):
    tokens, local = x.shape
    hw = min(2 * HD, local)
    return pl.pallas_call(
        forward_body,
        grid_spec=pltpu.PrefetchScalarGridSpec(
            num_scalar_prefetch=1,
            grid=(local // hw,),
            in_specs=attention_specs(tokens, hw),
            out_specs=pl.BlockSpec((tokens, hw), lambda h, ids: (0, h)),
        ),
        out_shape=jax.ShapeDtypeStruct((tokens, local), BF16),
        compiler_params=params("arbitrary"),
        cost_estimate=cost(12 * tokens * tokens * local, 10 * tokens * local),
    )(ids, proj, proj, proj, x)


def attend_backward(ids, proj, c, scale):
    tokens, local = c.shape
    hw = min(2 * HD, local)
    return pl.pallas_call(
        backward_body,
        grid_spec=pltpu.PrefetchScalarGridSpec(
            num_scalar_prefetch=1,
            grid=(local // hw,),
            in_specs=attention_specs(tokens, hw)
            + [pl.BlockSpec((tokens, 1), lambda h, ids: (0, 0))],
            out_specs=[
                pl.BlockSpec((3, tokens, hw), lambda h, ids: (0, 0, h)),
                pl.BlockSpec((tokens, HD), lambda h, ids: (0, 0)),
            ],
            scratch_shapes=[pltpu.VMEM((hw // HD, tokens, HD), F32) for _ in range(2)],
        ),
        out_shape=[
            jax.ShapeDtypeStruct((3, tokens, local), BF16),
            jax.ShapeDtypeStruct((tokens, HD), F32),
        ],
        compiler_params=params("arbitrary"),
        cost_estimate=cost(24 * tokens * tokens * local, 14 * tokens * local),
    )(ids, proj, proj, proj, c, scale)


def grad_in_body(ids_ref, grads_ref, w_ref, out_ref):
    total = lax.dot_general(grads_ref[0], w_ref[0], NT, preferred_element_type=F32)
    for k in (1, 2):
        total += lax.dot_general(grads_ref[k], w_ref[k], NT, preferred_element_type=F32)
    out_ref[0] = total.astype(out_ref.dtype)


def grad_in_blocks(ids, grads, w3, out_type):
    tokens, local = grads.shape[1:]
    count = ids.shape[0]
    ft = min(512, local)
    steps = local // ft
    return pl.pallas_call(
        grad_in_body,
        grid_spec=pltpu.PrefetchScalarGridSpec(
            num_scalar_prefetch=1,
            grid=(count, steps),
            in_specs=[
                pl.BlockSpec((3, tokens, local), lambda i, j, ids: (0, 0, 0)),
                pl.BlockSpec((3, ft, local), lambda i, j, ids: (0, ids[i] * steps + j, 0)),
            ],
            out_specs=pl.BlockSpec((1, tokens, ft), lambda i, j, ids: (i, 0, j)),
        ),
        out_shape=jax.ShapeDtypeStruct((count, tokens, local), out_type),
        compiler_params=params("arbitrary", "arbitrary"),
        cost_estimate=cost(6 * tokens * count * local * local, 6 * count * local * local),
    )(ids, grads, w3)


def grad_w_body(ids_ref, *refs):
    grads_ref, out_ref = refs[-2:]
    for i, x_ref in enumerate(refs[:-2]):

        @pl.when(pl.program_id(0) == i)
        def _():
            ft = out_ref.shape[1]
            start = pl.multiple_of(pl.program_id(1) * ft, ft)
            flipped = x_ref[:, pl.ds(start, ft)].T
            for k in range(3):
                out = jnp.dot(flipped, grads_ref[k], preferred_element_type=F32)
                out_ref[k] = out.astype(BF16)


def grad_weight(ids, blocks, grads):
    _, tokens, local = grads.shape
    count = len(blocks)
    ft = min(1024, local)
    steps = local // ft
    return pl.pallas_call(
        grad_w_body,
        grid_spec=pltpu.PrefetchScalarGridSpec(
            num_scalar_prefetch=1,
            grid=(count, steps),
            in_specs=[pl.BlockSpec((tokens, local), lambda i, j, ids: (0, 0)) for _ in blocks]
            + [pl.BlockSpec((3, tokens, local), lambda i, j, ids: (0, 0, 0))],
            out_specs=pl.BlockSpec((3, ft, local), lambda i, j, ids: (0, ids[i] * steps + j, 0)),
        ),
        out_shape=jax.ShapeDtypeStruct((3, count * local, local), BF16),
        compiler_params=params("arbitrary", "arbitrary"),
        cost_estimate=project_cost(tokens, count, local),
    )(ids, *blocks, grads)


def shifted(block, axis, distance):
    n = lax.axis_size(axis)
    return lax.ppermute(block, axis, [((i - distance) % n, i) for i in range(n)])


def swap_core(block):
    return lax.ppermute(block, "fsdp", [(i, i ^ 1) for i in range(lax.axis_size("fsdp"))])


def next_chip(block, distance):
    n = lax.axis_size("fsdp")
    route = [(i, ((i // 2 + distance) % (n // 2)) * 2 + i % 2) for i in range(n)]
    return lax.ppermute(block, "fsdp", route)


def summed(block):
    total = block
    for distance in range(1, lax.axis_size("fsdp")):
        total += shifted(block, "fsdp", distance)
    return total


def on_device(x_fwd, x_saved, cotangent, qkv_weight, gain, block_lists, plan):
    forward_in, saved_in, upstream = x_fwd[0], x_saved[0], cotangent[0]
    gain_row = gain[0][None, :]
    w3 = jnp.transpose(qkv_weight[0], (1, 0, 2))
    full_width, local = w3.shape[1:]
    tokens = forward_in.shape[0]
    n = lax.axis_size("fsdp")
    chips = n // 2
    me = lax.axis_index("fsdp").astype(jnp.int32)
    chip, core = lax.shift_right_logical(me, 1), me & 1
    wrap = lambda c: jnp.where(c < 0, c + chips, jnp.where(c >= chips, c - chips, c))
    near_ids = jnp.stack([me, me ^ 1])
    source = [wrap(chip - d) * 2 + core for d in range(1, chips)]
    far_ids = jnp.stack([i for s in source for i in (s, s ^ 1)])

    wide_fwd = forward_in.astype(F32)
    wide_bwd = saved_in.astype(F32)
    scaled_bwd = (wide_bwd * gain_row).astype(BF16)
    scaled_fwd = (wide_fwd * gain_row).astype(BF16)
    squares = jnp.stack([jnp.sum(wide_fwd * wide_fwd, axis=1), jnp.sum(wide_bwd * wide_bwd, axis=1)])
    both = jnp.concatenate([scaled_bwd, scaled_fwd], axis=0)

    sibling = swap_core(both)
    far_bwd = [next_chip(scaled_bwd, d) for d in range(1, chips)]
    scales = lax.rsqrt(summed(squares) / full_width + EPS)
    scale_fwd, scale_bwd = scales[0][:, None], scales[1][:, None]
    near = project_near(near_ids, [both, sibling], w3)

    scaled_fwd, far_bwd, near = lax.optimization_barrier((scaled_fwd, far_bwd, near))
    far_bwd = [x for block in far_bwd for x in (block, swap_core(block))]
    far_fwd = [next_chip(scaled_fwd, d) for d in range(1, chips)]
    proj_bwd = project_far(far_ids, far_bwd, w3, near, 0, scale_bwd)
    grads, totals = attend_backward(block_lists[plan[0, 1]], proj_bwd, upstream, scale_bwd)
    totals = summed(jnp.sum(totals, axis=1))

    others = jnp.arange(chips, dtype=jnp.int32)
    theirs = grad_in_blocks(others * 2 + 1 - core, grads, w3, BF16)
    far_fwd, theirs, later = lax.optimization_barrier((far_fwd, theirs, grads))
    far_fwd = [x for block in far_fwd for x in (block, swap_core(block))]
    from_core = swap_core(theirs)
    target = [wrap(chip + d) for d in range(1, chips)]
    far_part = grad_in_blocks(jnp.stack([t * 2 + core for t in target]), later, w3, F32)
    sends = []
    for d in range(1, chips):
        here = lax.dynamic_index_in_dim(from_core, target[d - 1], 0, keepdims=False)
        sends.append((far_part[d - 1] + here.astype(F32)).astype(BF16))
    sends, later, from_core = lax.optimization_barrier((sends, later, from_core))
    arrived = [next_chip(block, d) for d, block in enumerate(sends, 1)]
    own_in = grad_in_blocks(me[None], later, w3, F32)[0]
    own_in, near = lax.optimization_barrier((own_in, near))
    own_in += lax.dynamic_index_in_dim(from_core, chip, 0, keepdims=False).astype(F32)

    proj_fwd = project_far(far_ids, far_fwd, w3, near, 1, scale_fwd)
    result = attend_forward(block_lists[plan[0, 0]], proj_fwd, forward_in)
    sent_on = shifted(result[None], "section", 1)

    for block in arrived:
        own_in += block.astype(F32)
    grad_x = upstream.astype(F32) + gain_row * own_in
    grad_x = grad_x - scale_bwd * (totals / full_width)[:, None] * wide_bwd
    sent_back = shifted(grad_x.astype(BF16)[None], "section", -1)
    grad_gain = jnp.sum(wide_bwd * own_in, axis=0)[None]
    all_ids = jnp.concatenate([near_ids, far_ids])
    grad_w = grad_weight(all_ids, [both, sibling, *far_bwd], grads)
    return (sent_on, sent_back, jnp.transpose(grad_w, (1, 0, 2))[None], grad_gain)


def solution(mesh):
    in_specs = (
        P("section", None, "fsdp"),
        P("section", None, "fsdp"),
        P("section", None, "fsdp"),
        P("section", None, None, "fsdp"),
        P("section", "fsdp"),
        P(),
        P("section", None),
    )
    out_specs = (
        P("section", None, "fsdp"),
        P("section", None, "fsdp"),
        P("section", None, None, "fsdp"),
        P("section", "fsdp"),
    )
    return jax.shard_map(
        on_device, mesh=mesh, in_specs=in_specs, out_specs=out_specs, check_vma=False
    )
```

time: 170 us -> 174 us (1.024)
  between operations: 18.2 us -> 4.85 us
  blocking collectives: 11.3 us -> 0 us
  starting transfers between devices: 5.45 us -> 14.3 us
  local copies, waits for them, and re-layouts: 6.74 us -> 14.1 us
  waiting for transfers between devices: 24.7 us -> 30.3 us
  Pallas kernels: 95 us -> 99.1 us
  other arithmetic: 8.23 us -> 10.3 us
    ppermute x2 -> x8, waiting for transfers between devices: 4.68 us -> 30.3 us  [shifted(): lax.ppermute(block, axis, [((i - distance) % n, i) for i in range(n)])]
    all_gather x2 -> x0, waiting for transfers between devices: 19.3 us -> none  [the longest x1 19.3 us: on_device(): whole_bwd = lax.all_gather(scaled_bwd, 'fsdp', axis=1, tiled=True)]
    all_gather x2 -> x0, blocking collectives: 11.3 us -> none  [the longest x1 6.19 us: on_device(): squares = jnp.sum(lax.all_gather(squares, 'fsdp'), axis=0)]
    unnamed x23 -> x48, local copies, waits for them, and re-layouts: 5.58 us -> 11.1 us
    ppermute x2 -> x7, starting transfers between devices: 0.65 us -> 6 us  [the longest x3 4.17 us: next_chip(): return lax.ppermute(block, 'fsdp', route)]
    pallas_call x5 -> x6, Pallas kernels: 75.5 us -> 79.3 us  [the longest x2 25.9 us: project_far(): pl.pallas_call(far_body, grid_spec=pltpu.PrefetchScalarGridSpec(num_scala...]
    ppermute x2 -> x8, starting transfers between devices: 4.72 us -> 8.27 us  [shifted(): lax.ppermute(block, axis, [((i - distance) % n, i) for i in range(n)])]
    reduce_sum x3 -> x2, other arithmetic: 0.18 us -> 2.46 us  [the longest x1 2.31 us: on_device(): jnp.sum(wide_bwd * wide_bwd, axis=1)]
  transfers between devices with their start and end apart: 6 -> 15, of which waited for: 3 -> 4; matrix products, arithmetic and copies ran while one was open for 4% -> 5% of each run, Pallas kernels for 56% -> 57%
where the time goes in v1:
time: 174 us; the launch traced here: 173 us
  Pallas kernels  99.1 us (57%)
  waiting for transfers between devices  30.3 us (17%)
  starting transfers between devices  14.3 us (8%)
  local copies, waits for them, and re-layouts  14.1 us (8%)
  other arithmetic  10.3 us (6%)
  between operations  4.85 us (3%)
    ppermute x8, waiting for transfers between devices, shifted(): lax.ppermute(block, axis, [((i - distance) % n, i) for i in range(n)])  30.3 us
    pallas_call x2, Pallas kernels, project_far(): pl.pallas_call(far_body, grid_spec=pltpu.PrefetchScalarGridSpec(num_scala...  25.9 us
    pallas_call x3, Pallas kernels, grad_in_blocks(): pl.pallas_call(grad_in_body, grid_spec=pltpu.PrefetchScalarGridSpec(num_s...  19.8 us
    pallas_call x1, Pallas kernels, grad_weight(): pl.pallas_call(grad_w_body, grid_spec=pltpu.PrefetchScalarGridSpec(num_sc...  18.4 us
    pallas_call x1, Pallas kernels, project_near(): pl.pallas_call(near_body, grid_spec=pltpu.PrefetchScalarGridSpec(num_scal...  15.3 us
    unnamed x48, local copies, waits for them, and re-layouts  11.1 us
    pallas_call x1, Pallas kernels, attend_backward(): pl.pallas_call(backward_body, grid_spec=pltpu.PrefetchScalarGridSpec(num_...  11 us
    pallas_call x1, Pallas kernels, attend_forward(): pl.pallas_call(forward_body, grid_spec=pltpu.PrefetchScalarGridSpec(num_s...  8.82 us
  transfers between devices with their start and end apart: 15, of which 4 were waited for; matrix products, arithmetic and copies ran while one was open for 5% of the time, Pallas kernels for 57%

profile of v1, /device:TPU:0, one launch (start us, length us, event | category | flops | bytes accessed | tf_op | source)
XLA Modules:
  0.0 173.0 jit_solution(17756979421694349174)
XLA Ops:
  0.7 2.3 %fusion.3 = (f32[384]{0:T(512)S(1)}, bf16[384,1024]{1,0:T(8,128)(2,1)}) fusion(bf16[1,384,1024]{2,1,0:T(8,128)(2,1)} %param.8, f32[1024]{0:T(1024)} %bitcast.61), kind=kLoop, calls=%fused_computation.9 | loop fusion | flops 1965696 | bytes 1578496 | tf_op jit(solution)/shard_map/reduce_sum | solution.py:320
  4.1 1.5 pad_maximum_fusion.refs_0_
  6.1 2.6 %collective-permute-start = (bf16[384,1024]{1,0:T(8,128)(2,1)}, bf16[384,1024]{1,0:T(8,128)(2,1)}, u32[]{:S(2)}, u32[]{:S(2)}) collective-permute-start(bf16[384,1024]{1,0:T(8,128)(2,1)} %get-tuple-element.35), channel_id=1, source_target_pairs={{0,2},{1,3},{2,0},{3,1},{4,6},{5,7},{6,4},{7,5},{8,10},{9,11},{10,... | collective-permute-start | bytes 2359304 | tf_op jit(solution)/shard_map/ppermute | solution.py:291
  8.8 1.5 collective-permute-start.6
  11.0 15.3 %shard_map.102.refs_4_ = f32[3,768,1024]{2,1,0:T(8,128)S(1)} custom-call(s32[2]{0:T(128)S(1)} %pad_add_fusion.1.ids_ref, bf16[768,1024]{1,0:T(8,128)(2,1)S(1)} %pad_maximum_fusion.refs_0_, bf16[768,1024]{1,0:T(8,128)(2,1)S(1)} %collective-permute-done.1.refs_1_, bf16[3,4096,1024]{2,1,0:T(8,128)(2,1)} %bitcast.51, bf16[3,4096,1024]{2,1,0:T(8,128)(2,1)} %bitcast.52), custom_call_target="tpu_custom_call" | custom-call | flops 603979776 | bytes 786432 | tf_op jit(solution)/shard_map/pallas_call | solution.py:64
  26.3 3.7 %copy-done = f32[3,768,1024]{2,1,0:T(8,128)} copy-done((f32[3,768,1024]{2,1,0:T(8,128)}, f32[3,768,1024]{2,1,0:T(8,128)S(1)}, u32[]{:S(2)}) %copy-start) | copy-done | bytes 9437208
  38.1 3.7 %copy-done.1 = f32[3,768,1024]{2,1,0:T(8,128)S(1)} copy-done((f32[3,768,1024]{2,1,0:T(8,128)S(1)}, f32[3,768,1024]{2,1,0:T(8,128)}, u32[]{:S(2)}) %copy-start.1) | copy-done | bytes 9437208
  41.7 12.8 %shard_map.103.q_ref.k_ref.v_ref = bf16[3,384,1024]{2,1,0:T(8,128)(2,1)S(1)} custom-call(s32[2]{0:T(128)S(1)} %pad_add_fusion.ids_ref, bf16[384,1024]{1,0:T(8,128)(2,1)} %collective-permute-done.refs_0_.refs_2_, bf16[384,1024]{1,0:T(8,128)(2,1)S(1)} %collective-permute-done.3.refs_1_.refs_3_, bf16[3,4096,1024]{2,1,0:T(8,128)(2,1)} %bitcast.53, ...), custom_call_target="tpu_custom_call" | custom-call | flops 301989888 | bytes 786432 | tf_op jit(solution)/shard_map/pallas_call | solution.py:82
  54.6 11.0 %shard_map.104 = (bf16[3,384,1024]{2,1,0:T(8,128)(2,1)S(1)}, f32[384,128]{1,0:T(8,128)S(1)}) custom-call(s32[3,2]{1,0:T(4,128)S(1)} %copy.18.ids_ref, bf16[3,384,1024]{2,1,0:T(8,128)(2,1)S(1)} %shard_map.103.q_ref.k_ref.v_ref, bf16[3,384,1024]{2,1,0:T(8,128)(2,1)S(1)} %shard_map.103.q_ref.k_ref.v_ref, ...), custom_call_target="tpu_custom_call" | custom-call | flops 226492416 | bytes 344064 | tf_op jit(solution)/shard_map/pallas_call | solution.py:194
  65.5 10.0 %shard_map.105 = bf16[2,384,1024]{2,1,0:T(8,128)(2,1)} custom-call(s32[2]{0:T(128)S(1)} %add_subtract_fusion.ids_ref, bf16[3,384,1024]{2,1,0:T(8,128)(2,1)S(1)} %get-tuple-element.24.grads_ref.refs_4_, bf16[3,4096,1024]{2,1,0:T(8,128)(2,1)} %bitcast.55), custom_call_target="tpu_custom_call" | custom-call | flops 301989888 | bytes 786432 | tf_op jit(solution)/shard_map/pallas_call | solution.py:228
  76.1 4.8 %shard_map.106 = f32[1,384,1024]{2,1,0:T(8,128)S(1)} custom-call(s32[1]{0:T(128)} %bitcast.17.ids_ref, bf16[3,384,1024]{2,1,0:T(8,128)(2,1)S(1)} %get-tuple-element.24.grads_ref.refs_4_, bf16[3,4096,1024]{2,1,0:T(8,128)(2,1)} %bitcast.56), custom_call_target="tpu_custom_call" | custom-call | flops 150994944 | bytes 393216 | tf_op jit(solution)/shard_map/pallas_call | solution.py:228
  80.9 2.3 %fusion.8 = bf16[384,1024]{1,0:T(8,128)(2,1)} fusion(f32[1,384,1024]{2,1,0:T(8,128)S(1)} %shard_map.106, bf16[2,384,1024]{2,1,0:T(8,128)(2,1)} %collective-permute-done.8, s32[]{:T(128)S(6)} %select_n.32), kind=kLoop, calls=%fused_computation.17 | loop fusion | flops 1179648 | bytes 3145732 | tf_op jit(solution)/shard_map/convert_element_type | solution.py:346
  86.0 15.2 %collective-permute-done.13 = f32[384]{0:T(512)S(1)} collective-permute-done((f32[384]{0:T(512)S(1)}, f32[384]{0:T(512)S(1)}, u32[]{:S(2)}, u32[]{:S(2)}) %collective-permute-start.13) | collective-permute-done | bytes 1568 | tf_op jit(solution)/shard_map/ppermute | solution.py:281
  101.2 1.9 %collective-permute-done.12 = f32[384]{0:T(512)S(1)} collective-permute-done((f32[384]{0:T(512)S(1)}, f32[384]{0:T(512)S(1)}, u32[]{:S(2)}, u32[]{:S(2)}) %collective-permute-start.12) | collective-permute-done | bytes 1568 | tf_op jit(solution)/shard_map/ppermute | solution.py:281
  103.1 1.8 %copy-done.3 = bf16[3,384,1024]{2,1,0:T(8,128)(2,1)S(1)} copy-done((bf16[3,384,1024]{2,1,0:T(8,128)(2,1)S(1)}, bf16[3,384,1024]{2,1,0:T(8,128)(2,1)}, u32[]{:S(2)}) %copy-start.3) | copy-done | bytes 2359320
  104.9 5.0 %shard_map.107 = f32[1,384,1024]{2,1,0:T(8,128)S(1)} custom-call(s32[1]{0:T(128)} %bitcast.7.ids_ref, bf16[3,384,1024]{2,1,0:T(8,128)(2,1)S(1)} %copy-done.3, bf16[3,4096,1024]{2,1,0:T(8,128)(2,1)} %bitcast.57), custom_call_target="tpu_custom_call" | custom-call | flops 150994944 | bytes 393216 | tf_op jit(solution)/shard_map/pallas_call | solution.py:228
  110.0 13.1 %shard_map.108.q_ref.k_ref.v_ref = bf16[3,384,1024]{2,1,0:T(8,128)(2,1)S(1)} custom-call(s32[2]{0:T(128)S(1)} %pad_add_fusion.ids_ref, bf16[384,1024]{1,0:T(8,128)(2,1)} %collective-permute-done.2.refs_0_, bf16[384,1024]{1,0:T(8,128)(2,1)} %collective-permute-done.7.refs_1_, bf16[3,4096,1024]{2,1,0:T(8,128)(2,1)} %bitcast.58, ...), custom_call_target="tpu_custom_call" | custom-call | flops 301989888 | bytes 786432 | tf_op jit(solution)/shard_map/pallas_call | solution.py:82
  123.1 8.8 %shard_map.109 = bf16[384,1024]{1,0:T(8,128)(2,1)S(1)} custom-call(s32[3,2]{1,0:T(4,128)S(1)} %copy.21.ids_ref, bf16[3,384,1024]{2,1,0:T(8,128)(2,1)S(1)} %shard_map.108.q_ref.k_ref.v_ref, bf16[3,384,1024]{2,1,0:T(8,128)(2,1)S(1)} %shard_map.108.q_ref.k_ref.v_ref, bf16[3,384,1024]{2,1,0:T(8,128)(2,1)S(1)} %shard_map.108.q_ref.k_ref.v_ref, ...), custom_call_target="tpu_custom_call" | custom-call | flops 113246208 | bytes 245760 | tf_op jit(solution)/shard_map/pallas_call | solution.py:177
  132.0 1.6 collective-permute-start.9
  133.5 2.7 %fusion.6 = (f32[1024]{0:T(1024)}, bf16[1,384,1024]{2,1,0:T(8,128)(2,1)S(1)}) fusion(bf16[1,384,1024]{2,1,0:T(8,128)(2,1)S(1)} %copy-done.13, bf16[384,1024]{1,0:T(8,128)(2,1)} %collective-permute-done.10, f32[384,1024]{1,0:T(8,128)S(1)} %bitcast.47, bf16[2,384,1024]{2,1,0:T(8,128)(2,1)} %collective-permute-done.8, s32[]{:T(128)S(6)} %select_n.33, ...), kind=kLoop, calls=%fused_computation.12 | loop fusion | flops 5110784 | bytes 5514756 | tf_op jit(solution)/shard_map/reduce_sum | solution.py:362
  136.2 3.3 %collective-permute-start.14 = (bf16[1,384,1024]{2,1,0:T(8,128)(2,1)S(1)}, bf16[1,384,1024]{2,1,0:T(8,128)(2,1)S(1)}, u32[]{:S(2)}, u32[]{:S(2)}) collective-permute-start(bf16[1,384,1024]{2,1,0:T(8,128)(2,1)S(1)} %get-tuple-element.31), channel_id=1, source_target_pairs={{4,0},{8,4},{12,8},{16,12},{20,16},{24,20},{28,24},{0,28},{5,1},{9... | collective-permute-start | bytes 2359304 | tf_op jit(solution)/shard_map/ppermute | solution.py:281
  139.7 18.4 %shard_map.110 = bf16[3,4096,1024]{2,1,0:T(8,128)(2,1)} custom-call(s32[4]{0:T(128)S(1)} %pad_add_fusion.2.ids_ref, bf16[768,1024]{1,0:T(8,128)(2,1)S(1)} %copy-done.6, bf16[768,1024]{1,0:T(8,128)(2,1)S(1)} %copy-done.8, bf16[384,1024]{1,0:T(8,128)(2,1)} %collective-permute-done.refs_0_.refs_2_, ...), custom_call_target="tpu_custom_call" | custom-call | flops 603979776 | bytes 1572864 | tf_op jit(solution)/shard_map/pallas_call | solution.py:264
  158.0 9.5 %collective-permute-done.9 = bf16[1,384,1024]{2,1,0:T(8,128)(2,1)S(1)} collective-permute-done((bf16[1,384,1024]{2,1,0:T(8,128)(2,1)S(1)}, bf16[1,384,1024]{2,1,0:T(8,128)(2,1)S(1)}, u32[]{:S(2)}, u32[]{:S(2)}) %collective-permute-start.9) | collective-permute-done | bytes 786464 | tf_op jit(solution)/shard_map/ppermute | solution.py:281
  167.5 3.8 %collective-permute-done.14 = bf16[1,384,1024]{2,1,0:T(8,128)(2,1)S(1)} collective-permute-done((bf16[1,384,1024]{2,1,0:T(8,128)(2,1)S(1)}, bf16[1,384,1024]{2,1,0:T(8,128)(2,1)S(1)}, u32[]{:S(2)}, u32[]{:S(2)}) %collective-permute-start.14) | collective-permute-done | bytes 786464 | tf_op jit(solution)/shard_map/ppermute | solution.py:281
  (88 shorter events, 11.8 us)
Async XLA Ops:
  5.6 20.7 %copy-start.5 = (bf16[768,1024]{1,0:T(8,128)(2,1)}, bf16[768,1024]{1,0:T(8,128)(2,1)S(1)}, u32[]{:S(2)}) copy-start(bf16[768,1024]{1,0:T(8,128)(2,1)S(1)} %pad_maximum_fusion.refs_0_) | copy-start | bytes 4718596
  5.6 5.4 %collective-permute-start.1 = (bf16[768,1024]{1,0:T(8,128)(2,1)S(1)}, bf16[768,1024]{1,0:T(8,128)(2,1)S(1)}, u32[]{:S(2)}, u32[]{:S(2)}) collective-permute-start(bf16[768,1024]{1,0:T(8,128)(2,1)S(1)} %pad_maximum_fusion.refs_0_), channel_id=1, source_target_pairs={{0,1},{1,0},{2,3},{3,2},{4,5},{5,4},{6,7},{7,6},{8,9},{9,8},{10,11... | collective-permute-start | bytes 4718600 | tf_op jit(solution)/shard_map/ppermute | solution.py:285
  6.1 23.9 %collective-permute-start = (bf16[384,1024]{1,0:T(8,128)(2,1)}, bf16[384,1024]{1,0:T(8,128)(2,1)}, u32[]{:S(2)}, u32[]{:S(2)}) collective-permute-start(bf16[384,1024]{1,0:T(8,128)(2,1)} %get-tuple-element.35), channel_id=1, source_target_pairs={{0,2},{1,3},{2,0},{3,1},{4,6},{5,7},{6,4},{7,5},{8,10},{9,11},{10,... | collective-permute-start | bytes 2359304 | tf_op jit(solution)/shard_map/ppermute | solution.py:291
  8.7 28.0 %collective-permute-start.5 = (f32[2,384]{1,0:T(2,128)S(1)}, f32[2,384]{1,0:T(2,128)S(1)}, u32[]{:S(2)}, u32[]{:S(2)}) collective-permute-start(f32[2,384]{1,0:T(2,128)S(1)} %pad_maximum_fusion.1), channel_id=1, source_target_pairs={{2,0},{3,1},{0,2},{1,3},{6,4},{7,5},{4,6},{5,7},{10,8},{11,9},{8,1... | collective-permute-start | bytes 9224 | tf_op jit(solution)/shard_map/ppermute | solution.py:281
  8.8 27.9 %collective-permute-start.6 = (f32[2,384]{1,0:T(2,128)S(1)}, f32[2,384]{1,0:T(2,128)S(1)}, u32[]{:S(2)}, u32[]{:S(2)}) collective-permute-start(f32[2,384]{1,0:T(2,128)S(1)} %pad_maximum_fusion.1), channel_id=1, source_target_pairs={{1,0},{2,1},{3,2},{0,3},{5,4},{6,5},{7,6},{4,7},{9,8},{10,9},{11,1... | collective-permute-start | bytes 9224 | tf_op jit(solution)/shard_map/ppermute | solution.py:281
  10.3 26.4 %collective-permute-start.4 = (f32[2,384]{1,0:T(2,128)S(1)}, f32[2,384]{1,0:T(2,128)S(1)}, u32[]{:S(2)}, u32[]{:S(2)}) collective-permute-start(f32[2,384]{1,0:T(2,128)S(1)} %pad_maximum_fusion.1), channel_id=1, source_target_pairs={{3,0},{0,1},{1,2},{2,3},{7,4},{4,5},{5,6},{6,7},{11,8},{8,9},{9,10... | collective-permute-start | bytes 9224 | tf_op jit(solution)/shard_map/ppermute | solution.py:281
  11.0 15.3 %copy-start.7 = (bf16[768,1024]{1,0:T(8,128)(2,1)}, bf16[768,1024]{1,0:T(8,128)(2,1)S(1)}, u32[]{:S(2)}) copy-start(bf16[768,1024]{1,0:T(8,128)(2,1)S(1)} %collective-permute-done.1.refs_1_) | copy-start | bytes 4718596
  11.0 24.8 %copy-start.15 = (s32[8,3,2]{0,2,1:T(2,128)S(1)}, s32[8,3,2]{0,2,1:T(2,128)}, u32[]{:S(2)}) copy-start(s32[8,3,2]{0,2,1:T(2,128)} %param.12) | copy-start | bytes 580
  30.0 45.5 %collective-permute-start.2 = (bf16[384,1024]{1,0:T(8,128)(2,1)}, bf16[384,1024]{1,0:T(8,128)(2,1)}, u32[]{:S(2)}, u32[]{:S(2)}) collective-permute-start(bf16[384,1024]{1,0:T(8,128)(2,1)} %get-tuple-element.17), channel_id=1, source_target_pairs={{0,2},{1,3},{2,0},{3,1},{4,6},{5,7},{6,4},{7,5},{8,10},{9,11},{10,... | collective-permute-start | bytes 2359304 | tf_op jit(solution)/shard_map/ppermute | solution.py:291
  31.1 7.0 %collective-permute-start.3 = (bf16[384,1024]{1,0:T(8,128)(2,1)}, bf16[384,1024]{1,0:T(8,128)(2,1)S(1)}, u32[]{:S(2)}, u32[]{:S(2)}) collective-permute-start(bf16[384,1024]{1,0:T(8,128)(2,1)} %collective-permute-done.refs_0_.refs_2_), channel_id=1, source_target_pairs={{0,1},{1,0},{2,3},{3,2},{4,5},{5,4},{6,7},{7,6},{8,9},{9,8},{10,11... | collective-permute-start | bytes 2359304 | tf_op jit(solution)/shard_map/ppermute | solution.py:285
  41.7 12.8 %copy-start.11 = (bf16[1,384,1024]{2,1,0:T(8,128)(2,1)S(1)}, bf16[1,384,1024]{2,1,0:T(8,128)(2,1)}, u32[]{:S(2)}) copy-start(bf16[1,384,1024]{2,1,0:T(8,128)(2,1)} %param.9) | copy-start | bytes 2359300
  65.5 10.5 %copy-start.2 = (bf16[3,384,1024]{2,1,0:T(8,128)(2,1)}, bf16[3,384,1024]{2,1,0:T(8,128)(2,1)S(1)}, u32[]{:S(2)}) copy-start(bf16[3,384,1024]{2,1,0:T(8,128)(2,1)S(1)} %get-tuple-element.24.grads_ref.refs_4_) | copy-start | bytes 7077892
  75.5 5.4 %collective-permute-start.8 = (bf16[2,384,1024]{2,1,0:T(8,128)(2,1)}, bf16[2,384,1024]{2,1,0:T(8,128)(2,1)}, u32[]{:S(2)}, u32[]{:S(2)}) collective-permute-start(bf16[2,384,1024]{2,1,0:T(8,128)(2,1)} %shard_map.105), channel_id=1, source_target_pairs={{0,1},{1,0},{2,3},{3,2},{4,5},{5,4},{6,7},{7,6},{8,9},{9,8},{10,11... | collective-permute-start | bytes 4718600 | tf_op jit(solution)/shard_map/ppermute | solution.py:285
  75.6 34.4 %collective-permute-start.7 = (bf16[384,1024]{1,0:T(8,128)(2,1)}, bf16[384,1024]{1,0:T(8,128)(2,1)}, u32[]{:S(2)}, u32[]{:S(2)}) collective-permute-start(bf16[384,1024]{1,0:T(8,128)(2,1)} %collective-permute-done.2.refs_0_), channel_id=1, source_target_pairs={{0,1},{1,0},{2,3},{3,2},{4,5},{5,4},{6,7},{7,6},{8,9},{9,8},{10,11... | collective-permute-start | bytes 2359304 | tf_op jit(solution)/shard_map/ppermute | solution.py:285
  80.9 22.2 %copy-start.17 = (f32[384]{0:T(512)S(1)}, f32[384]{0:T(512)}, u32[]{:S(2)}) copy-start(f32[384]{0:T(512)} %get-tuple-element.36) | copy-start | bytes 4612
  83.2 50.3 %collective-permute-start.10 = (bf16[384,1024]{1,0:T(8,128)(2,1)}, bf16[384,1024]{1,0:T(8,128)(2,1)}, u32[]{:S(2)}, u32[]{:S(2)}) collective-permute-start(bf16[384,1024]{1,0:T(8,128)(2,1)} %fusion.8), channel_id=1, source_target_pairs={{0,2},{1,3},{2,0},{3,1},{4,6},{5,7},{6,4},{7,5},{8,10},{9,11},{10,... | collective-permute-start | bytes 2359304 | tf_op jit(solution)/shard_map/ppermute | solution.py:291
  83.9 17.3 %collective-permute-start.13 = (f32[384]{0:T(512)S(1)}, f32[384]{0:T(512)S(1)}, u32[]{:S(2)}, u32[]{:S(2)}) collective-permute-start(f32[384]{0:T(512)S(1)} %reduce_sum.38), channel_id=1, source_target_pairs={{1,0},{2,1},{3,2},{0,3},{5,4},{6,5},{7,6},{4,7},{9,8},{10,9},{11,1... | collective-permute-start | bytes 4616 | tf_op jit(solution)/shard_map/ppermute | solution.py:281
  84.8 18.3 %collective-permute-start.12 = (f32[384]{0:T(512)S(1)}, f32[384]{0:T(512)S(1)}, u32[]{:S(2)}, u32[]{:S(2)}) collective-permute-start(f32[384]{0:T(512)S(1)} %reduce_sum.38), channel_id=1, source_target_pairs={{2,0},{3,1},{0,2},{1,3},{6,4},{7,5},{4,6},{5,7},{10,8},{11,9},{8,1... | collective-permute-start | bytes 4616 | tf_op jit(solution)/shard_map/ppermute | solution.py:281
  85.5 17.6 %collective-permute-start.11 = (f32[384]{0:T(512)S(1)}, f32[384]{0:T(512)S(1)}, u32[]{:S(2)}, u32[]{:S(2)}) collective-permute-start(f32[384]{0:T(512)S(1)} %reduce_sum.38), channel_id=1, source_target_pairs={{3,0},{0,1},{1,2},{2,3},{7,4},{4,5},{5,6},{6,7},{11,8},{8,9},{9,10... | collective-permute-start | bytes 4616 | tf_op jit(solution)/shard_map/ppermute | solution.py:281
  109.9 13.1 %copy-start.10 = (bf16[1,384,1024]{2,1,0:T(8,128)(2,1)S(1)}, bf16[1,384,1024]{2,1,0:T(8,128)(2,1)}, u32[]{:S(2)}) copy-start(bf16[1,384,1024]{2,1,0:T(8,128)(2,1)} %param.7) | copy-start | bytes 2359300
  123.1 10.5 %copy-start.12 = (bf16[1,384,1024]{2,1,0:T(8,128)(2,1)S(1)}, bf16[1,384,1024]{2,1,0:T(8,128)(2,1)}, u32[]{:S(2)}) copy-start(bf16[1,384,1024]{2,1,0:T(8,128)(2,1)} %param.9) | copy-start | bytes 2359300
  123.1 10.4 %copy-start.13 = (bf16[1,384,1024]{2,1,0:T(8,128)(2,1)S(1)}, bf16[1,384,1024]{2,1,0:T(8,128)(2,1)}, u32[]{:S(2)}) copy-start(bf16[1,384,1024]{2,1,0:T(8,128)(2,1)} %param.8) | copy-start | bytes 2359300
  132.0 35.5 %collective-permute-start.9 = (bf16[1,384,1024]{2,1,0:T(8,128)(2,1)S(1)}, bf16[1,384,1024]{2,1,0:T(8,128)(2,1)S(1)}, u32[]{:S(2)}, u32[]{:S(2)}) collective-permute-start(bf16[1,384,1024]{2,1,0:T(8,128)(2,1)S(1)} %bitcast.50), channel_id=1, source_target_pairs={{28,0},{0,4},{4,8},{8,12},{12,16},{16,20},{20,24},{24,28},{29,1},{... | collective-permute-start | bytes 2359304 | tf_op jit(solution)/shard_map/ppermute | solution.py:281
  136.2 35.0 %collective-permute-start.14 = (bf16[1,384,1024]{2,1,0:T(8,128)(2,1)S(1)}, bf16[1,384,1024]{2,1,0:T(8,128)(2,1)S(1)}, u32[]{:S(2)}, u32[]{:S(2)}) collective-permute-start(bf16[1,384,1024]{2,1,0:T(8,128)(2,1)S(1)} %get-tuple-element.31), channel_id=1, source_target_pairs={{4,0},{8,4},{12,8},{16,12},{20,16},{24,20},{28,24},{0,28},{5,1},{9... | collective-permute-start | bytes 2359304 | tf_op jit(solution)/shard_map/ppermute | solution.py:281
  (14 other events, 70.0 us)

commit v2 on v1

--- a/solution.py
+++ b/solution.py
@@ -1,3 +1,4 @@
+import functools
 import math
 
 import jax
@@ -12,15 +13,16 @@
 EPS = 1e-05
 INV = 1.0 / math.sqrt(HD)
 LOG2E = math.log2(math.e)
-VMEM = 40 * 1024 * 1024
+VMEM = 28 * 1024 * 1024
 F32 = jnp.float32
 BF16 = jnp.bfloat16
 NT = (((1,), (1,)), ((), ()))
 TN = (((0,), (0,)), ((), ()))
+TICK = jax.ShapeDtypeStruct((8, 128), jnp.int32)
 
 
 def cost(flops, moved):
-    return pl.CostEstimate(flops=flops // 16, bytes_accessed=moved // 16, transcendentals=0)
+    return pl.CostEstimate(flops=flops // 1024, bytes_accessed=moved // 1024, transcendentals=0)
 
 
 def params(*sem):
@@ -35,14 +37,17 @@
 
 
 def near_body(ids_ref, *refs):
-    count = (len(refs) - 1) // 2
-    refs[-1][0] = total_of(refs[:count], refs[count:-1])
+    out_ref, tick_ref = refs[-2:]
+    count = (len(refs) - 2) // 2
+    tick_ref[...] = jnp.zeros_like(tick_ref)
+    out_ref[0] = total_of(refs[:count], refs[count:-2]).astype(BF16)
 
 
 def far_body(ids_ref, *refs):
-    acc_ref, scale_ref, out_ref = refs[-3:]
-    count = (len(refs) - 3) // 2
-    product = acc_ref[0] + total_of(refs[:count], refs[count:-3])
+    acc_ref, scale_ref, out_ref, tick_ref = refs[-4:]
+    count = (len(refs) - 4) // 2
+    tick_ref[...] = jnp.zeros_like(tick_ref)
+    product = acc_ref[0].astype(F32) + total_of(refs[:count], refs[count:-4])
     out_ref[0] = (scale_ref[...] * product).astype(BF16)
 
 
@@ -67,9 +72,12 @@
             num_scalar_prefetch=1,
             grid=(3, local // nt),
             in_specs=operand_specs(count, tokens, local, nt),
-            out_specs=pl.BlockSpec((1, tokens, nt), lambda k, j, ids: (k, 0, j)),
-        ),
-        out_shape=jax.ShapeDtypeStruct((3, tokens, local), F32),
+            out_specs=[
+                pl.BlockSpec((1, tokens, nt), lambda k, j, ids: (k, 0, j)),
+                pl.BlockSpec((8, 128), lambda k, j, ids: (0, 0)),
+            ],
+        ),
+        out_shape=[jax.ShapeDtypeStruct((3, tokens, local), BF16), TICK],
         compiler_params=params("arbitrary", "arbitrary"),
         cost_estimate=project_cost(tokens, count, local),
     )(ids, *blocks, *[w3] * count)
@@ -89,17 +97,25 @@
                 pl.BlockSpec((1, tokens, nt), lambda k, j, ids: (k, half, j)),
                 pl.BlockSpec((tokens, 1), lambda k, j, ids: (0, 0)),
             ],
-            out_specs=pl.BlockSpec((1, tokens, nt), lambda k, j, ids: (k, 0, j)),
-        ),
-        out_shape=jax.ShapeDtypeStruct((3, tokens, local), BF16),
+            out_specs=[
+                pl.BlockSpec((1, tokens, nt), lambda k, j, ids: (k, 0, j)),
+                pl.BlockSpec((8, 128), lambda k, j, ids: (0, 0)),
+            ],
+        ),
+        out_shape=[jax.ShapeDtypeStruct((3, tokens, local), BF16), TICK],
         compiler_params=params("arbitrary", "arbitrary"),
         cost_estimate=project_cost(tokens, count, local),
     )(ids, *blocks, *[w3] * count, acc, scale)
 
 
-def probs_of(q_b, key_a, key_b):
-    s_a = lax.dot_general(key_a, q_b, NT, preferred_element_type=F32)
-    s_b = lax.dot_general(key_b, q_b, NT, preferred_element_type=F32)
+def scores_of(left_a, left_b, right):
+    return (
+        lax.dot_general(left_a, right, NT, preferred_element_type=F32),
+        lax.dot_general(left_b, right, NT, preferred_element_type=F32),
+    )
+
+
+def probs_of(s_a, s_b):
     top = jnp.max(jnp.maximum(s_a, s_b), axis=0, keepdims=True)
     e_a = jnp.exp2((s_a - top) * (INV * LOG2E))
     e_b = jnp.exp2((s_b - top) * (INV * LOG2E))
@@ -107,23 +123,26 @@
     return e_a * share, e_b * share
 
 
-def other_rows(ids_ref, b):
-    return pl.ds(pl.multiple_of(ids_ref[b, 1] * BLK, BLK), BLK)
+def units_of(ids_ref, tokens, cols):
+    units = []
+    for h in range(cols // HD):
+        for b in range(tokens // BLK):
+            other = pl.ds(pl.multiple_of(ids_ref[b, 1] * BLK, BLK), BLK)
+            units.append((h, slice(h * HD, (h + 1) * HD), slice(b * BLK, (b + 1) * BLK), other))
+    return units
 
 
 def forward_body(ids_ref, q_ref, k_ref, v_ref, x_ref, out_ref):
-    tokens, cols = x_ref.shape
-    for h in range(cols // HD):
-        hs = slice(h * HD, (h + 1) * HD)
-        for b in range(tokens // BLK):
-            bs = slice(b * BLK, (b + 1) * BLK)
-            other = other_rows(ids_ref, b)
-            p_a, p_b = probs_of(q_ref[0, bs, hs], k_ref[0, bs, hs], k_ref[0, other, hs])
-            attn = lax.dot_general(p_a.astype(BF16), v_ref[0, bs, hs], TN, preferred_element_type=F32)
-            attn += lax.dot_general(
-                p_b.astype(BF16), v_ref[0, other, hs], TN, preferred_element_type=F32
-            )
-            out_ref[bs, hs] = (x_ref[bs, hs].astype(F32) + attn).astype(BF16)
+    units = units_of(ids_ref, *x_ref.shape)
+    scores = [
+        scores_of(k_ref[0, bs, hs], k_ref[0, other, hs], q_ref[0, bs, hs])
+        for _, hs, bs, other in units
+    ]
+    probs = [[p.astype(BF16) for p in probs_of(*pair)] for pair in scores]
+    for (_, hs, bs, other), (p_a, p_b) in zip(units, probs):
+        attn = lax.dot_general(p_a, v_ref[0, bs, hs], TN, preferred_element_type=F32)
+        attn += lax.dot_general(p_b, v_ref[0, other, hs], TN, preferred_element_type=F32)
+        out_ref[bs, hs] = (x_ref[bs, hs].astype(F32) + attn).astype(BF16)
 
 
 def backward_body(ids_ref, q_ref, k_ref, v_ref, c_ref, scale_ref, grads_ref, total_ref, gk_ref, gv_ref):
@@ -133,37 +152,52 @@
     def _():
         total_ref[...] = jnp.zeros_like(total_ref)
 
+    units = units_of(ids_ref, tokens, cols)
+    scores = [
+        scores_of(k_ref[0, bs, hs], k_ref[0, other, hs], q_ref[0, bs, hs])
+        for _, hs, bs, other in units
+    ]
+    grad_ps = [
+        scores_of(v_ref[0, bs, hs], v_ref[0, other, hs], c_ref[bs, hs])
+        for _, hs, bs, other in units
+    ]
+    lows = []
+    for pair, (gp_a, gp_b) in zip(scores, grad_ps):
+        p_a, p_b = probs_of(*pair)
+        inner = jnp.sum(p_a * gp_a + p_b * gp_b, axis=0, keepdims=True)
+        gs_a = (p_a * (gp_a - inner) * INV).astype(BF16)
+        gs_b = (p_b * (gp_b - inner) * INV).astype(BF16)
+        lows.append((p_a.astype(BF16), p_b.astype(BF16), gs_a, gs_b))
+    later = []
+    grad_qs = []
+    for (h, hs, bs, other), (p_a, p_b, gs_a, gs_b) in zip(units, lows):
+        q_b, c_b = q_ref[0, bs, hs], c_ref[bs, hs]
+        gv_ref[h, bs, :] = jnp.dot(p_a, c_b, preferred_element_type=F32)
+        gk_ref[h, bs, :] = jnp.dot(gs_a, q_b, preferred_element_type=F32)
+        grad_q = lax.dot_general(gs_a, k_ref[0, bs, hs], TN, preferred_element_type=F32)
+        grad_q += lax.dot_general(gs_b, k_ref[0, other, hs], TN, preferred_element_type=F32)
+        grad_qs.append((scale_ref[bs, :] * grad_q).astype(BF16))
+        later.append(
+            (
+                jnp.dot(p_b, c_b, preferred_element_type=F32),
+                jnp.dot(gs_b, q_b, preferred_element_type=F32),
+            )
+        )
+    for (h, _, _, other), (more_v, more_k) in zip(units, later):
+        gv_ref[h, other, :] += more_v
+        gk_ref[h, other, :] += more_k
+    for (_, hs, bs, _), grad_q in zip(units, grad_qs):
+        grads_ref[0, bs, hs] = grad_q
+        total_ref[bs, :] += grad_q.astype(F32) * q_ref[0, bs, hs].astype(F32)
     for h in range(cols // HD):
         hs = slice(h * HD, (h + 1) * HD)
-        later = []
-        for b in range(tokens // BLK):
-            bs = slice(b * BLK, (b + 1) * BLK)
-            other = other_rows(ids_ref, b)
-            q_b, c_b = q_ref[0, bs, hs], c_ref[bs, hs]
-            key_a, key_b = k_ref[0, bs, hs], k_ref[0, other, hs]
-            p_a, p_b = probs_of(q_b, key_a, key_b)
-            gp_a = lax.dot_general(v_ref[0, bs, hs], c_b, NT, preferred_element_type=F32)
-            gp_b = lax.dot_general(v_ref[0, other, hs], c_b, NT, preferred_element_type=F32)
-            inner = jnp.sum(p_a * gp_a + p_b * gp_b, axis=0, keepdims=True)
-            gs_a = (p_a * (gp_a - inner) * INV).astype(BF16)
-            gs_b = (p_b * (gp_b - inner) * INV).astype(BF16)
-            gv_ref[h, bs, :] = jnp.dot(p_a.astype(BF16), c_b, preferred_element_type=F32)
-            gk_ref[h, bs, :] = jnp.dot(gs_a, q_b, preferred_element_type=F32)
-            later.append((other, p_b.astype(BF16), c_b, gs_b, q_b))
-            grad_q = lax.dot_general(gs_a, key_a, TN, preferred_element_type=F32)
-            grad_q += lax.dot_general(gs_b, key_b, TN, preferred_element_type=F32)
-            grad_q = (scale_ref[bs, :] * grad_q).astype(BF16)
-            grads_ref[0, bs, hs] = grad_q
-            total_ref[bs, :] += grad_q.astype(F32) * q_b.astype(F32)
-        for other, p_b, c_b, gs_b, q_b in later:
-            gv_ref[h, other, :] += jnp.dot(p_b, c_b, preferred_element_type=F32)
-            gk_ref[h, other, :] += jnp.dot(gs_b, q_b, preferred_element_type=F32)
         grad_k = (scale_ref[...] * gk_ref[h]).astype(BF16)
         grad_v = (scale_ref[...] * gv_ref[h]).astype(BF16)
         grads_ref[1, :, hs] = grad_k
         grads_ref[2, :, hs] = grad_v
-        total_ref[...] += grad_k.astype(F32) * k_ref[0, :, hs].astype(F32)
-        total_ref[...] += grad_v.astype(F32) * v_ref[0, :, hs].astype(F32)
+        total_ref[...] += grad_k.astype(F32) * k_ref[0, :, hs].astype(F32) + grad_v.astype(
+            F32
+        ) * v_ref[0, :, hs].astype(F32)
 
 
 def attention_specs(tokens, hw):
@@ -242,9 +276,9 @@
     )(ids, grads, w3)
 
 
-def grad_w_body(ids_ref, *refs):
+def grad_w_body(count, ids_ref, *refs):
     grads_ref, out_ref = refs[-2:]
-    for i, x_ref in enumerate(refs[:-2]):
+    for i, x_ref in enumerate(refs[-2 - count : -2]):
 
         @pl.when(pl.program_id(0) == i)
         def _():
@@ -256,24 +290,26 @@
                 out_ref[k] = out.astype(BF16)
 
 
-def grad_weight(ids, blocks, grads):
+def grad_weight(ids, blocks, grads, width, begun=()):
     _, tokens, local = grads.shape
     count = len(blocks)
-    ft = min(1024, local)
+    ft = min(512, local)
     steps = local // ft
     return pl.pallas_call(
-        grad_w_body,
+        functools.partial(grad_w_body, count),
         grid_spec=pltpu.PrefetchScalarGridSpec(
             num_scalar_prefetch=1,
             grid=(count, steps),
-            in_specs=[pl.BlockSpec((tokens, local), lambda i, j, ids: (0, 0)) for _ in blocks]
+            in_specs=[pl.BlockSpec(memory_space=pl.ANY) for _ in begun]
+            + [pl.BlockSpec((tokens, local), lambda i, j, ids: (0, 0)) for _ in blocks]
             + [pl.BlockSpec((3, tokens, local), lambda i, j, ids: (0, 0, 0))],
             out_specs=pl.BlockSpec((3, ft, local), lambda i, j, ids: (0, ids[i] * steps + j, 0)),
         ),
-        out_shape=jax.ShapeDtypeStruct((3, count * local, local), BF16),
+        out_shape=jax.ShapeDtypeStruct((3, width, local), BF16),
         compiler_params=params("arbitrary", "arbitrary"),
         cost_estimate=project_cost(tokens, count, local),
-    )(ids, *blocks, grads)
+        input_output_aliases={1: 0} if begun else {},
+    )(ids, *begun, *blocks, grads)
 
 
 def shifted(block, axis, distance):
@@ -291,11 +327,8 @@
     return lax.ppermute(block, "fsdp", route)
 
 
-def summed(block):
-    total = block
-    for distance in range(1, lax.axis_size("fsdp")):
-        total += shifted(block, "fsdp", distance)
-    return total
+def all_parts(block):
+    return [block] + [shifted(block, "fsdp", d) for d in range(1, lax.axis_size("fsdp"))]
 
 
 def on_device(x_fwd, x_saved, cotangent, qkv_weight, gain, block_lists, plan):
@@ -322,16 +355,17 @@
 
     sibling = swap_core(both)
     far_bwd = [next_chip(scaled_bwd, d) for d in range(1, chips)]
-    scales = lax.rsqrt(summed(squares) / full_width + EPS)
+    scales = lax.rsqrt(sum(all_parts(squares)) / full_width + EPS)
     scale_fwd, scale_bwd = scales[0][:, None], scales[1][:, None]
-    near = project_near(near_ids, [both, sibling], w3)
-
-    scaled_fwd, far_bwd, near = lax.optimization_barrier((scaled_fwd, far_bwd, near))
+    near, tick = project_near(near_ids, [both, sibling], w3)
+
+    scaled_fwd, far_bwd, tick = lax.optimization_barrier((scaled_fwd, far_bwd, tick))
+    far_ids = far_ids + tick[0, 0]
     far_bwd = [x for block in far_bwd for x in (block, swap_core(block))]
     far_fwd = [next_chip(scaled_fwd, d) for d in range(1, chips)]
-    proj_bwd = project_far(far_ids, far_bwd, w3, near, 0, scale_bwd)
+    proj_bwd, _ = project_far(far_ids, far_bwd, w3, near, 0, scale_bwd)
     grads, totals = attend_backward(block_lists[plan[0, 1]], proj_bwd, upstream, scale_bwd)
-    totals = summed(jnp.sum(totals, axis=1))
+    totals = all_parts(jnp.sum(totals, axis=1))
 
     others = jnp.arange(chips, dtype=jnp.int32)
     theirs = grad_in_blocks(others * 2 + 1 - core, grads, w3, BF16)
@@ -344,24 +378,26 @@
     for d in range(1, chips):
         here = lax.dynamic_index_in_dim(from_core, target[d - 1], 0, keepdims=False)
         sends.append((far_part[d - 1] + here.astype(F32)).astype(BF16))
-    sends, later, from_core = lax.optimization_barrier((sends, later, from_core))
+    sends, later, scale_fwd = lax.optimization_barrier((sends, later, scale_fwd))
     arrived = [next_chip(block, d) for d, block in enumerate(sends, 1)]
     own_in = grad_in_blocks(me[None], later, w3, F32)[0]
-    own_in, near = lax.optimization_barrier((own_in, near))
     own_in += lax.dynamic_index_in_dim(from_core, chip, 0, keepdims=False).astype(F32)
 
-    proj_fwd = project_far(far_ids, far_fwd, w3, near, 1, scale_fwd)
-    result = attend_forward(block_lists[plan[0, 0]], proj_fwd, forward_in)
-    sent_on = shifted(result[None], "section", 1)
-
+    proj_fwd, tick = project_far(far_ids, far_fwd, w3, near, 1, scale_fwd)
+    arrived, totals, tick = lax.optimization_barrier((arrived, totals, tick))
     for block in arrived:
         own_in += block.astype(F32)
     grad_x = upstream.astype(F32) + gain_row * own_in
-    grad_x = grad_x - scale_bwd * (totals / full_width)[:, None] * wide_bwd
-    sent_back = shifted(grad_x.astype(BF16)[None], "section", -1)
+    grad_x = grad_x - scale_bwd * (sum(totals) / full_width)[:, None] * wide_bwd
+    lists_fwd = block_lists[plan[0, 0]] + tick[0, 0]
+    grad_x, lists_fwd = lax.optimization_barrier((grad_x.astype(BF16), lists_fwd))
+    sent_back = shifted(grad_x[None], "section", -1)
+    result = attend_forward(lists_fwd, proj_fwd, forward_in)
     grad_gain = jnp.sum(wide_bwd * own_in, axis=0)[None]
-    all_ids = jnp.concatenate([near_ids, far_ids])
-    grad_w = grad_weight(all_ids, [both, sibling, *far_bwd], grads)
+    begun = grad_weight(near_ids, [both, sibling], grads, full_width)
+    sent_back, begun, result = lax.optimization_barrier((sent_back, begun, result))
+    sent_on = shifted(result[None], "section", 1)
+    grad_w = grad_weight(far_ids, far_bwd, grads, full_width, [begun])
     return (sent_on, sent_back, jnp.transpose(grad_w, (1, 0, 2))[None], grad_gain)
 
 

time: 174 us -> 156 us (0.90)
  waiting for transfers between devices: 30.3 us -> 13.4 us
  Pallas kernels: 99.1 us -> 92.2 us
  local copies, waits for them, and re-layouts: 14.1 us -> 18.4 us
    ppermute x8, waiting for transfers between devices: 30.3 us -> 13.4 us  [shifted(): lax.ppermute(block, axis, [((i - distance) % n, i) for i in range(n)])]
    pallas_call x1, Pallas kernels: 8.82 us -> 3.86 us  [attend_forward(): pl.pallas_call(forward_body, grid_spec=pltpu.PrefetchScalarGridSpec(num_s...]
    pallas_call x1, Pallas kernels: 11 us -> 6.81 us  [attend_backward(): pl.pallas_call(backward_body, grid_spec=pltpu.PrefetchScalarGridSpec(num_...]
    reduce_sum x3 -> x1, other arithmetic: 3.56 us -> 0.14 us  [on_device(): totals = all_parts(jnp.sum(totals, axis=1))]
    convert_element_type x0 -> x1, other arithmetic: none -> 2.72 us  [on_device(): scaled_bwd = (wide_bwd * gain_row).astype(BF16)]
    unnamed x48 -> x41, local copies, waits for them, and re-layouts: 11.1 us -> 13.6 us
    pallas_call x1 -> x2, Pallas kernels: 18.4 us -> 20.5 us  [grad_weight(): pl.pallas_call(functools.partial(grad_w_body, count), grid_spec=pltpu.Pre...]
  transfers between devices with their start and end apart: 15 -> 15, of which waited for: 4 -> 2; matrix products, arithmetic and copies ran while one was open for 5% -> 5% of each run, Pallas kernels for 57% -> 59%
where the time goes in v2:
time: 156 us; the launch traced here: 155 us
  Pallas kernels  92.2 us (59%)
  local copies, waits for them, and re-layouts  18.4 us (12%)
  starting transfers between devices  14.6 us (9%)
  waiting for transfers between devices  13.4 us (9%)
  other arithmetic  11.7 us (8%)
  between operations  4.59 us (3%)
    pallas_call x2, Pallas kernels, project_far(): pl.pallas_call(far_body, grid_spec=pltpu.PrefetchScalarGridSpec(num_scala...  26.4 us
    pallas_call x2, Pallas kernels, grad_weight(): pl.pallas_call(functools.partial(grad_w_body, count), grid_spec=pltpu.Pre...  20.5 us
    pallas_call x3, Pallas kernels, grad_in_blocks(): pl.pallas_call(grad_in_body, grid_spec=pltpu.PrefetchScalarGridSpec(num_s...  19.4 us
    pallas_call x1, Pallas kernels, project_near(): pl.pallas_call(near_body, grid_spec=pltpu.PrefetchScalarGridSpec(num_scal...  15.2 us
    unnamed x41, local copies, waits for them, and re-layouts  13.6 us
    ppermute x8, waiting for transfers between devices, shifted(): lax.ppermute(block, axis, [((i - distance) % n, i) for i in range(n)])  13.4 us
    ppermute x8, starting transfers between devices, shifted(): lax.ppermute(block, axis, [((i - distance) % n, i) for i in range(n)])  8.26 us
    pallas_call x1, Pallas kernels, attend_backward(): pl.pallas_call(backward_body, grid_spec=pltpu.PrefetchScalarGridSpec(num_...  6.81 us
  transfers between devices with their start and end apart: 15, of which 2 were waited for; matrix products, arithmetic and copies ran while one was open for 5% of the time, Pallas kernels for 59%

profile of v2, /device:TPU:0, one launch (start us, length us, event | category | flops | bytes accessed | tf_op | source)
XLA Modules:
  0.0 154.9 jit_solution(7465276062369911373)
XLA Ops:
  0.6 2.7 %fusion.2 = (bf16[384,1024]{1,0:T(8,128)(2,1)}, f32[384]{0:T(512)S(1)}, f32[384]{0:T(512)S(1)}, bf16[384,1024]{1,0:T(8,128)(2,1)S(1)}) fusion(bf16[1,384,1024]{2,1,0:T(8,128)(2,1)} %param.8, f32[1024]{0:T(1024)} %bitcast.58, bf16[1,384,1024]{2,1,0:T(8,128)(2,1)} %param.7), kind=kLoop, calls=%fused_computation.8 | loop fusion | flops 3931392 | bytes 3152896 | tf_op jit(solution)/shard_map/convert_element_type | solution.py:351
  6.0 2.6 %collective-permute-start = (bf16[384,1024]{1,0:T(8,128)(2,1)}, bf16[384,1024]{1,0:T(8,128)(2,1)}, u32[]{:S(2)}, u32[]{:S(2)}) collective-permute-start(bf16[384,1024]{1,0:T(8,128)(2,1)} %get-tuple-element.60), channel_id=1, source_target_pairs={{0,2},{1,3},{2,0},{3,1},{4,6},{5,7},{6,4},{7,5},{8,10},{9,11},{10,... | collective-permute-start | bytes 2359304 | tf_op jit(solution)/shard_map/ppermute | solution.py:327
  8.7 1.5 collective-permute-start.6
  13.4 15.2 %shard_map.102 = (bf16[3,768,1024]{2,1,0:T(8,128)(2,1)S(1)}, s32[8,128]{1,0:T(8,128)S(1)}) custom-call(s32[2]{0:T(128)S(1)} %pad_add_fusion.ids_ref, bf16[768,1024]{1,0:T(8,128)(2,1)S(1)} %pad_maximum_fusion.refs_0_, bf16[768,1024]{1,0:T(8,128)(2,1)S(1)} %collective-permute-done.1.refs_1_, bf16[3,4096,1024]{2,1,0:T(8,128)(2,1)} %bitcast.48, ...), custom_call_target="tpu_custom_call" | custom-call | flops 9437184 | bytes 12288 | tf_op jit(solution)/shard_map/pallas_call | solution.py:69
  28.6 2.2 %copy-done.2 = bf16[3,768,1024]{2,1,0:T(8,128)(2,1)} copy-done((bf16[3,768,1024]{2,1,0:T(8,128)(2,1)}, bf16[3,768,1024]{2,1,0:T(8,128)(2,1)S(1)}, u32[]{:S(2)}) %copy-start.2) | copy-done | bytes 4718616
  32.6 1.6 %collective-permute-start.2 = (bf16[384,1024]{1,0:T(8,128)(2,1)}, bf16[384,1024]{1,0:T(8,128)(2,1)}, u32[]{:S(2)}, u32[]{:S(2)}) collective-permute-start(bf16[384,1024]{1,0:T(8,128)(2,1)} %copy-done.12), channel_id=1, source_target_pairs={{0,2},{1,3},{2,0},{3,1},{4,6},{5,7},{6,4},{7,5},{8,10},{9,11},{10,... | collective-permute-start | bytes 2359304 | tf_op jit(solution)/shard_map/ppermute | solution.py:327
  37.7 2.3 %copy-done.3 = bf16[3,768,1024]{2,1,0:T(8,128)(2,1)S(1)} copy-done((bf16[3,768,1024]{2,1,0:T(8,128)(2,1)S(1)}, bf16[3,768,1024]{2,1,0:T(8,128)(2,1)}, u32[]{:S(2)}) %copy-start.3) | copy-done | bytes 4718616
  40.1 13.4 %shard_map.103 = (bf16[3,384,1024]{2,1,0:T(8,128)(2,1)S(1)}, s32[8,128]{1,0:T(8,128)}) custom-call(s32[2]{0:T(128)S(1)} %add_add_fusion.ids_ref, bf16[384,1024]{1,0:T(8,128)(2,1)} %collective-permute-done.refs_0_.refs_1_, bf16[384,1024]{1,0:T(8,128)(2,1)S(1)} %collective-permute-done.3.refs_1_.refs_2_, bf16[3,4096,1024]{2,1,0:T(8,128)(2,1)} %bitcast.50, ...), custom_call_target="tpu_custom_call" | custom-call | flops 4718592 | bytes 12288 | tf_op jit(solution)/shard_map/pallas_call | solution.py:90
  53.5 6.8 %shard_map.104 = (bf16[3,384,1024]{2,1,0:T(8,128)(2,1)S(1)}, f32[384,128]{1,0:T(8,128)S(1)}) custom-call(s32[3,2]{1,0:T(4,128)S(1)} %copy.25.ids_ref, bf16[3,384,1024]{2,1,0:T(8,128)(2,1)S(1)} %get-tuple-element.36.q_ref.k_ref.v_ref, bf16[3,384,1024]{2,1,0:T(8,128)(2,1)S(1)} %get-tuple-element.36.q_ref.k_ref.v_ref, ...), custom_call_target="tpu_custom_call" | custom-call | flops 3538944 | bytes 5376 | tf_op jit(solution)/shard_map/pallas_call | solution.py:228
  60.3 9.7 %shard_map.105 = bf16[2,384,1024]{2,1,0:T(8,128)(2,1)} custom-call(s32[2]{0:T(128)S(1)} %add_subtract_fusion.ids_ref, bf16[3,384,1024]{2,1,0:T(8,128)(2,1)S(1)} %get-tuple-element.40.grads_ref.refs_2_.refs_3_, bf16[3,4096,1024]{2,1,0:T(8,128)(2,1)} %bitcast.52), custom_call_target="tpu_custom_call" | custom-call | flops 4718592 | bytes 12288 | tf_op jit(solution)/shard_map/pallas_call | solution.py:262
  70.5 4.8 %shard_map.106 = f32[1,384,1024]{2,1,0:T(8,128)S(1)} custom-call(s32[1]{0:T(128)} %bitcast.3.ids_ref, bf16[3,384,1024]{2,1,0:T(8,128)(2,1)S(1)} %get-tuple-element.40.grads_ref.refs_2_.refs_3_, bf16[3,4096,1024]{2,1,0:T(8,128)(2,1)} %bitcast.53), custom_call_target="tpu_custom_call" | custom-call | flops 2359296 | bytes 6144 | tf_op jit(solution)/shard_map/pallas_call | solution.py:262
  75.4 2.3 %fusion.7 = bf16[384,1024]{1,0:T(8,128)(2,1)} fusion(f32[1,384,1024]{2,1,0:T(8,128)S(1)} %shard_map.106, bf16[2,384,1024]{2,1,0:T(8,128)(2,1)} %collective-permute-done.7, s32[]{:T(128)S(6)} %select_n.31), kind=kLoop, calls=%fused_computation.16 | loop fusion | flops 1179648 | bytes 3145732 | tf_op jit(solution)/shard_map/convert_element_type | solution.py:380
  81.0 4.9 %shard_map.107 = f32[1,384,1024]{2,1,0:T(8,128)S(1)} custom-call(s32[1]{0:T(128)} %bitcast.2.ids_ref, bf16[3,384,1024]{2,1,0:T(8,128)(2,1)S(1)} %get-tuple-element.40.grads_ref.refs_2_.refs_3_, bf16[3,4096,1024]{2,1,0:T(8,128)(2,1)} %bitcast.54), custom_call_target="tpu_custom_call" | custom-call | flops 2359296 | bytes 6144 | tf_op jit(solution)/shard_map/pallas_call | solution.py:262
  85.9 2.3 %copy-done.4 = bf16[3,768,1024]{2,1,0:T(8,128)(2,1)S(1)} copy-done((bf16[3,768,1024]{2,1,0:T(8,128)(2,1)S(1)}, bf16[3,768,1024]{2,1,0:T(8,128)(2,1)}, u32[]{:S(2)}) %copy-start.4) | copy-done | bytes 4718616
  88.2 13.1 %shard_map.108 = (bf16[3,384,1024]{2,1,0:T(8,128)(2,1)S(1)}, s32[8,128]{1,0:T(8,128)S(1)}) custom-call(s32[2]{0:T(128)S(1)} %add_add_fusion.ids_ref, bf16[384,1024]{1,0:T(8,128)(2,1)} %collective-permute-done.2.refs_0_, bf16[384,1024]{1,0:T(8,128)(2,1)} %collective-permute-done.12.refs_1_, bf16[3,4096,1024]{2,1,0:T(8,128)(2,1)} %bitcast.55, ...), custom_call_target="tpu_custom_call" | custom-call | flops 4718592 | bytes 12288 | tf_op jit(solution)/shard_map/pallas_call | solution.py:90
  102.7 3.8 %fusion.6 = (f32[1024]{0:T(1024)}, bf16[384,1024]{1,0:T(8,128)(2,1)}) fusion(bf16[1,384,1024]{2,1,0:T(8,128)(2,1)S(1)} %copy-done.13, bf16[384,1024]{1,0:T(8,128)(2,1)} %collective-permute-done.8, f32[1,384,1024]{2,1,0:T(8,128)S(1)} %shard_map.107, bf16[2,384,1024]{2,1,0:T(8,128)(2,1)} %collective-permute-done.7, s32[]{:T(128)S(6)} %select_n.32, ...), kind=kLoop, calls=%fused_computation.12 | loop fusion | flops 5110784 | bytes 5514756 | tf_op jit(solution)/shard_map/reduce_sum | solution.py:396
  106.5 4.5 %collective-permute-start.13 = (bf16[1,384,1024]{2,1,0:T(8,128)(2,1)}, bf16[1,384,1024]{2,1,0:T(8,128)(2,1)}, u32[]{:S(2)}, u32[]{:S(2)}) collective-permute-start(bf16[1,384,1024]{2,1,0:T(8,128)(2,1)} %bitcast.23), channel_id=1, source_target_pairs={{4,0},{8,4},{12,8},{16,12},{20,16},{24,20},{28,24},{0,28},{5,1},{9... | collective-permute-start | bytes 2359304 | tf_op jit(solution)/shard_map/ppermute | solution.py:317
  111.0 9.7 %shard_map.109.refs_0_ = bf16[3,4096,1024]{2,1,0:T(8,128)(2,1)} custom-call(s32[2]{0:T(128)S(1)} %pad_add_fusion.ids_ref, bf16[768,1024]{1,0:T(8,128)(2,1)S(1)} %copy-done.6, bf16[768,1024]{1,0:T(8,128)(2,1)S(1)} %copy-done.8, bf16[3,384,1024]{2,1,0:T(8,128)(2,1)S(1)} %get-tuple-element.40.grads_ref.refs_2_.refs_3_), custom_call_target="tpu_custom_call" | custom-call | flops 4718592 | bytes 12288 | tf_op jit(solution)/shard_map/pallas_call | solution.py:298
  120.8 1.7 %copy-done.1 = bf16[3,384,1024]{2,1,0:T(8,128)(2,1)S(1)} copy-done((bf16[3,384,1024]{2,1,0:T(8,128)(2,1)S(1)}, bf16[3,384,1024]{2,1,0:T(8,128)(2,1)}, u32[]{:S(2)}) %copy-start.1) | copy-done | bytes 2359320
  123.6 3.9 %shard_map.110 = bf16[384,1024]{1,0:T(8,128)(2,1)S(1)} custom-call(s32[3,2]{1,0:T(4,128)S(1)} %copy.29.ids_ref, bf16[3,384,1024]{2,1,0:T(8,128)(2,1)S(1)} %copy-done.1, bf16[3,384,1024]{2,1,0:T(8,128)(2,1)S(1)} %copy-done.1, bf16[3,384,1024]{2,1,0:T(8,128)(2,1)S(1)} %copy-done.1, bf16[384,1024]{1,0:T(8,128)(2,1)S(1)} %bitcast.45), custom_call_target="tpu_custom_call" | custom-call | flops 1769472 | bytes 3840 | tf_op jit(solution)/shard_map/pallas_call | solution.py:211
  127.5 1.5 collective-permute-done.13
  129.3 10.8 %shard_map.111 = bf16[3,4096,1024]{2,1,0:T(8,128)(2,1)} custom-call(s32[2]{0:T(128)S(1)} %add_add_fusion.ids_ref, bf16[3,4096,1024]{2,1,0:T(8,128)(2,1)} %shard_map.109.refs_0_, bf16[384,1024]{1,0:T(8,128)(2,1)} %collective-permute-done.refs_0_.refs_1_, bf16[384,1024]{1,0:T(8,128)(2,1)S(1)} %collective-permute-done.3.refs_1_.refs_2_, ...), custom_call_target="tpu_custom_call", output_to_operand_aliasing={{}: (1, {})} | custom-call | flops 4718592 | bytes 12288 | tf_op jit(solution)/shard_map/pallas_call | solution.py:298
  140.1 11.9 %collective-permute-done.14 = bf16[1,384,1024]{2,1,0:T(8,128)(2,1)S(1)} collective-permute-done((bf16[1,384,1024]{2,1,0:T(8,128)(2,1)S(1)}, bf16[1,384,1024]{2,1,0:T(8,128)(2,1)S(1)}, u32[]{:S(2)}, u32[]{:S(2)}) %collective-permute-start.14) | collective-permute-done | bytes 786464 | tf_op jit(solution)/shard_map/ppermute | solution.py:317
  152.8 2.1 %copy.35 = bf16[1,384,1024]{2,1,0:T(8,128)(2,1)} copy(bf16[1,384,1024]{2,1,0:T(8,128)(2,1)} %collective-permute-done.13) | data formatting | bytes 1572864
  (81 shorter events, 15.3 us)
Async XLA Ops:
  5.5 23.0 %copy-start.5 = (bf16[768,1024]{1,0:T(8,128)(2,1)}, bf16[768,1024]{1,0:T(8,128)(2,1)S(1)}, u32[]{:S(2)}) copy-start(bf16[768,1024]{1,0:T(8,128)(2,1)S(1)} %pad_maximum_fusion.refs_0_) | copy-start | bytes 4718596
  5.5 7.8 %collective-permute-start.1 = (bf16[768,1024]{1,0:T(8,128)(2,1)S(1)}, bf16[768,1024]{1,0:T(8,128)(2,1)S(1)}, u32[]{:S(2)}, u32[]{:S(2)}) collective-permute-start(bf16[768,1024]{1,0:T(8,128)(2,1)S(1)} %pad_maximum_fusion.refs_0_), channel_id=1, source_target_pairs={{0,1},{1,0},{2,3},{3,2},{4,5},{5,4},{6,7},{7,6},{8,9},{9,8},{10,11... | collective-permute-start | bytes 4718600 | tf_op jit(solution)/shard_map/ppermute | solution.py:321
  6.0 24.7 %collective-permute-start = (bf16[384,1024]{1,0:T(8,128)(2,1)}, bf16[384,1024]{1,0:T(8,128)(2,1)}, u32[]{:S(2)}, u32[]{:S(2)}) collective-permute-start(bf16[384,1024]{1,0:T(8,128)(2,1)} %get-tuple-element.60), channel_id=1, source_target_pairs={{0,2},{1,3},{2,0},{3,1},{4,6},{5,7},{6,4},{7,5},{8,10},{9,11},{10,... | collective-permute-start | bytes 2359304 | tf_op jit(solution)/shard_map/ppermute | solution.py:327
  8.6 26.4 %collective-permute-start.5 = (f32[2,384]{1,0:T(2,128)S(1)}, f32[2,384]{1,0:T(2,128)S(1)}, u32[]{:S(2)}, u32[]{:S(2)}) collective-permute-start(f32[2,384]{1,0:T(2,128)S(1)} %pad_maximum_fusion.1), channel_id=1, source_target_pairs={{2,0},{3,1},{0,2},{1,3},{6,4},{7,5},{4,6},{5,7},{10,8},{11,9},{8,1... | collective-permute-start | bytes 9224 | tf_op jit(solution)/shard_map/ppermute | solution.py:317
  8.7 26.3 %collective-permute-start.6 = (f32[2,384]{1,0:T(2,128)S(1)}, f32[2,384]{1,0:T(2,128)S(1)}, u32[]{:S(2)}, u32[]{:S(2)}) collective-permute-start(f32[2,384]{1,0:T(2,128)S(1)} %pad_maximum_fusion.1), channel_id=1, source_target_pairs={{1,0},{2,1},{3,2},{0,3},{5,4},{6,5},{7,6},{4,7},{9,8},{10,9},{11,1... | collective-permute-start | bytes 9224 | tf_op jit(solution)/shard_map/ppermute | solution.py:317
  10.2 24.8 %collective-permute-start.4 = (f32[2,384]{1,0:T(2,128)S(1)}, f32[2,384]{1,0:T(2,128)S(1)}, u32[]{:S(2)}, u32[]{:S(2)}) collective-permute-start(f32[2,384]{1,0:T(2,128)S(1)} %pad_maximum_fusion.1), channel_id=1, source_target_pairs={{3,0},{0,1},{1,2},{2,3},{7,4},{4,5},{5,6},{6,7},{11,8},{8,9},{9,10... | collective-permute-start | bytes 9224 | tf_op jit(solution)/shard_map/ppermute | solution.py:317
  13.3 15.2 %copy-start.7 = (bf16[768,1024]{1,0:T(8,128)(2,1)}, bf16[768,1024]{1,0:T(8,128)(2,1)S(1)}, u32[]{:S(2)}) copy-start(bf16[768,1024]{1,0:T(8,128)(2,1)S(1)} %collective-permute-done.1.refs_1_) | copy-start | bytes 4718596
  13.4 20.8 %copy-start.15 = (s32[8,3,2]{0,2,1:T(2,128)S(1)}, s32[8,3,2]{0,2,1:T(2,128)}, u32[]{:S(2)}) copy-start(s32[8,3,2]{0,2,1:T(2,128)} %param.12) | copy-start | bytes 580
  30.7 7.0 %collective-permute-start.3 = (bf16[384,1024]{1,0:T(8,128)(2,1)}, bf16[384,1024]{1,0:T(8,128)(2,1)S(1)}, u32[]{:S(2)}, u32[]{:S(2)}) collective-permute-start(bf16[384,1024]{1,0:T(8,128)(2,1)} %collective-permute-done.refs_0_.refs_1_), channel_id=1, source_target_pairs={{0,1},{1,0},{2,3},{3,2},{4,5},{5,4},{6,7},{7,6},{8,9},{9,8},{10,11... | collective-permute-start | bytes 2359304 | tf_op jit(solution)/shard_map/ppermute | solution.py:321
  32.6 37.4 %collective-permute-start.2 = (bf16[384,1024]{1,0:T(8,128)(2,1)}, bf16[384,1024]{1,0:T(8,128)(2,1)}, u32[]{:S(2)}, u32[]{:S(2)}) collective-permute-start(bf16[384,1024]{1,0:T(8,128)(2,1)} %copy-done.12), channel_id=1, source_target_pairs={{0,2},{1,3},{2,0},{3,1},{4,6},{5,7},{6,4},{7,5},{8,10},{9,11},{10,... | collective-permute-start | bytes 2359304 | tf_op jit(solution)/shard_map/ppermute | solution.py:327
  40.1 13.4 %copy-start.10 = (bf16[1,384,1024]{2,1,0:T(8,128)(2,1)S(1)}, bf16[1,384,1024]{2,1,0:T(8,128)(2,1)}, u32[]{:S(2)}) copy-start(bf16[1,384,1024]{2,1,0:T(8,128)(2,1)} %param.9) | copy-start | bytes 2359300
  70.0 5.4 %collective-permute-start.7 = (bf16[2,384,1024]{2,1,0:T(8,128)(2,1)}, bf16[2,384,1024]{2,1,0:T(8,128)(2,1)}, u32[]{:S(2)}, u32[]{:S(2)}) collective-permute-start(bf16[2,384,1024]{2,1,0:T(8,128)(2,1)} %shard_map.105), channel_id=1, source_target_pairs={{0,1},{1,0},{2,3},{3,2},{4,5},{5,4},{6,7},{7,6},{8,9},{9,8},{10,11... | collective-permute-start | bytes 4718600 | tf_op jit(solution)/shard_map/ppermute | solution.py:321
  70.0 15.9 %collective-permute-start.12 = (bf16[384,1024]{1,0:T(8,128)(2,1)}, bf16[384,1024]{1,0:T(8,128)(2,1)}, u32[]{:S(2)}, u32[]{:S(2)}) collective-permute-start(bf16[384,1024]{1,0:T(8,128)(2,1)} %collective-permute-done.2.refs_0_), channel_id=1, source_target_pairs={{0,1},{1,0},{2,3},{3,2},{4,5},{5,4},{6,7},{7,6},{8,9},{9,8},{10,11... | collective-permute-start | bytes 2359304 | tf_op jit(solution)/shard_map/ppermute | solution.py:321
  77.6 23.7 %collective-permute-start.8 = (bf16[384,1024]{1,0:T(8,128)(2,1)}, bf16[384,1024]{1,0:T(8,128)(2,1)}, u32[]{:S(2)}, u32[]{:S(2)}) collective-permute-start(bf16[384,1024]{1,0:T(8,128)(2,1)} %fusion.7), channel_id=1, source_target_pairs={{0,2},{1,3},{2,0},{3,1},{4,6},{5,7},{6,4},{7,5},{8,10},{9,11},{10,... | collective-permute-start | bytes 2359304 | tf_op jit(solution)/shard_map/ppermute | solution.py:327
  78.3 23.0 %collective-permute-start.11 = (f32[384]{0:T(512)S(1)}, f32[384]{0:T(512)S(1)}, u32[]{:S(2)}, u32[]{:S(2)}) collective-permute-start(f32[384]{0:T(512)S(1)} %reduce_sum.38), channel_id=1, source_target_pairs={{1,0},{2,1},{3,2},{0,3},{5,4},{6,5},{7,6},{4,7},{9,8},{10,9},{11,1... | collective-permute-start | bytes 4616 | tf_op jit(solution)/shard_map/ppermute | solution.py:317
  79.2 22.1 %collective-permute-start.10 = (f32[384]{0:T(512)S(1)}, f32[384]{0:T(512)S(1)}, u32[]{:S(2)}, u32[]{:S(2)}) collective-permute-start(f32[384]{0:T(512)S(1)} %reduce_sum.38), channel_id=1, source_target_pairs={{2,0},{3,1},{0,2},{1,3},{6,4},{7,5},{4,6},{5,7},{10,8},{11,9},{8,1... | collective-permute-start | bytes 4616 | tf_op jit(solution)/shard_map/ppermute | solution.py:317
  79.9 21.4 %collective-permute-start.9 = (f32[384]{0:T(512)S(1)}, f32[384]{0:T(512)S(1)}, u32[]{:S(2)}, u32[]{:S(2)}) collective-permute-start(f32[384]{0:T(512)S(1)} %reduce_sum.38), channel_id=1, source_target_pairs={{3,0},{0,1},{1,2},{2,3},{7,4},{4,5},{5,6},{6,7},{11,8},{8,9},{9,10... | collective-permute-start | bytes 4616 | tf_op jit(solution)/shard_map/ppermute | solution.py:317
  88.2 14.4 %copy-start.17 = (f32[384]{0:T(512)S(1)}, f32[384]{0:T(512)}, u32[]{:S(2)}) copy-start(f32[384]{0:T(512)} %get-tuple-element.69) | copy-start | bytes 4612
  88.2 14.4 %copy-start.11 = (bf16[1,384,1024]{2,1,0:T(8,128)(2,1)S(1)}, bf16[1,384,1024]{2,1,0:T(8,128)(2,1)}, u32[]{:S(2)}) copy-start(bf16[1,384,1024]{2,1,0:T(8,128)(2,1)} %param.9) | copy-start | bytes 2359300
  88.2 14.4 %copy-start.13 = (bf16[1,384,1024]{2,1,0:T(8,128)(2,1)S(1)}, bf16[1,384,1024]{2,1,0:T(8,128)(2,1)}, u32[]{:S(2)}) copy-start(bf16[1,384,1024]{2,1,0:T(8,128)(2,1)} %param.8) | copy-start | bytes 2359300
  88.2 14.4 %copy-start.14 = (f32[1,1024]{1,0:T(1,128)S(1)}, f32[1,1024]{1,0:T(1,128)}, u32[]{:S(2)}) copy-start(f32[1,1024]{1,0:T(1,128)} %param.11) | copy-start | bytes 12292
  102.7 8.3 %copy-start.6 = (bf16[768,1024]{1,0:T(8,128)(2,1)S(1)}, bf16[768,1024]{1,0:T(8,128)(2,1)}, u32[]{:S(2)}) copy-start(bf16[768,1024]{1,0:T(8,128)(2,1)} %copy-done.5) | copy-start | bytes 4718596
  106.5 22.5 %collective-permute-start.13 = (bf16[1,384,1024]{2,1,0:T(8,128)(2,1)}, bf16[1,384,1024]{2,1,0:T(8,128)(2,1)}, u32[]{:S(2)}, u32[]{:S(2)}) collective-permute-start(bf16[1,384,1024]{2,1,0:T(8,128)(2,1)} %bitcast.23), channel_id=1, source_target_pairs={{4,0},{8,4},{12,8},{16,12},{20,16},{24,20},{28,24},{0,28},{5,1},{9... | collective-permute-start | bytes 2359304 | tf_op jit(solution)/shard_map/ppermute | solution.py:317
  128.9 23.0 %collective-permute-start.14 = (bf16[1,384,1024]{2,1,0:T(8,128)(2,1)S(1)}, bf16[1,384,1024]{2,1,0:T(8,128)(2,1)S(1)}, u32[]{:S(2)}, u32[]{:S(2)}) collective-permute-start(bf16[1,384,1024]{2,1,0:T(8,128)(2,1)S(1)} %bitcast.47), channel_id=1, source_target_pairs={{28,0},{0,4},{4,8},{8,12},{12,16},{16,20},{20,24},{24,28},{29,1},{... | collective-permute-start | bytes 2359304 | tf_op jit(solution)/shard_map/ppermute | solution.py:317
  (10 other events, 34.8 us)
